TPU v7x, 32 devices: a whole 2x2x4 slice. The times are simulated.
32 devices in a mesh: wide: 16 (over z, y, core), narrow: 2 (over x).
Axes of the slice: x: 2, y: 2, z: 4, core: 2. Of those that a mesh axis runs over, the one named last changes fastest.
Arguments:
- tokens: bfloat16 [4096, 1024], P(('wide', 'narrow')), may hold values from -6 to 6
- cotangent: bfloat16 [4096, 1024], P(('wide', 'narrow')), may hold values from -6 to 6
- seq_lengths: int32 [16, 2], P('wide'), may hold values from 1 to 254, as said below
- bucket_map: int32 [128], replicated, may hold values from 0 to 31
- norm1_gain: float32 [1024], replicated, may hold values from 0.1 to 1.9
- norm1_bias: float32 [1024], replicated, may hold values from -3 to 3
- ema_rate: float32 [16, 1024], replicated, may hold values from 0.00390625 to 0.06
- ema_damp: float32 [16, 1024], replicated, may hold values from 0.5 to 1
- ema_in: float32 [16, 1024], replicated, may hold values from -6 to 6
- ema_out: float32 [16, 1024], replicated, may hold values from -1.5 to 1.5
- ema_skip: float32 [1024], replicated, may hold values from -6 to 6
- w_shared: bfloat16 [1024, 128], replicated, may hold values from -0.1875 to 0.1875
- qk_gain: float32 [2, 128], replicated, may hold values from -8 to 8
- qk_bias: float32 [2, 128], replicated, may hold values from -3 to 3
- rel_bias: float32 [32], replicated, may hold values from -4 to 4
- w_value: bfloat16 [1024, 2048], P(None, 'narrow'), may hold values from -0.1875 to 0.1875
- w_reset: bfloat16 [1024, 2048], P(None, 'narrow'), may hold values from -0.1875 to 0.1875
- w_mix: bfloat16 [2048, 1024], P('narrow'), may hold values from -0.5 to 0.5
- w_hidden: bfloat16 [1024, 1024], replicated, may hold values from -0.1875 to 0.1875
- w_update: bfloat16 [1024, 1024], replicated, may hold values from -0.1875 to 0.1875
- b_update: float32 [1024], replicated, may hold values from -4 to 4
- norm2_gain: float32 [1024], replicated, may hold values from 0.1 to 1.9
- norm2_bias: float32 [1024], replicated, may hold values from -3 to 3
- w_up: bfloat16 [1024, 4096], P(None, 'narrow'), may hold values from -0.1875 to 0.1875
- b_up: bfloat16 [4096], P('narrow'), may hold values from -3 to 3
- w_down: bfloat16 [4096, 1024], P('narrow'), may hold values from -0.09375 to 0.09375
Outputs:
- block_out: bfloat16 [4096, 1024], P(('wide', 'narrow'))
- grad_tokens: float32 [4096, 1024], P(('wide', 'narrow'))
- grad_norm1_gain: float32 [1024], replicated
- grad_norm1_bias: float32 [1024], replicated
- grad_ema_rate: float32 [16, 1024], replicated
- grad_ema_damp: float32 [16, 1024], replicated
- grad_ema_in: float32 [16, 1024], replicated
- grad_ema_out: float32 [16, 1024], replicated
- grad_ema_skip: float32 [1024], replicated
- grad_w_shared: float32 [1024, 128], replicated
- grad_qk_gain: float32 [2, 128], replicated
- grad_qk_bias: float32 [2, 128], replicated
- grad_rel_bias: float32 [32], replicated
- grad_w_value: float32 [1024, 2048], P(None, 'narrow')
- grad_w_reset: float32 [1024, 2048], P(None, 'narrow')
- grad_w_mix: float32 [2048, 1024], P('narrow')
- grad_w_hidden: float32 [1024, 1024], replicated
- grad_w_update: float32 [1024, 1024], replicated
- grad_b_update: float32 [1024], replicated
- grad_norm2_gain: float32 [1024], replicated
- grad_norm2_bias: float32 [1024], replicated
- grad_w_up: float32 [1024, 4096], P(None, 'narrow')
- grad_b_up: float32 [4096], P('narrow')
- grad_w_down: float32 [4096, 1024], P('narrow')
Inputs may be any that keep to these rules, and one draw needn't show every extreme that they name: `seq_lengths`: in each group the two lengths leave at least one position of padding at the group's end; one of the two sequences starts on the group's first device and ends on its last.
All inputs are finite; a program needn't handle non-finite values.
Results may differ from a plain program's by a relative error of at most 0.02.
The roundings to bfloat16 on the way count: a program that leaves them out, or rounds other values in their place, can miss the bound.
Values may be sent and summed in bfloat16 or wider, within the bound.
A program may use at most 384 MiB of HBM per device.

v0:
```python
import jax
import jax.numpy as jnp
from jax import lax
from jax.experimental import pallas as pl
from jax.experimental.pallas import tpu as pltpu
from jax.sharding import PartitionSpec as P

BLOCK = 128


EPSILON = 1e-05
NEGATIVE = -1000000000.0


def carried_in(part, axis, combine, identity, reverse):
    count = lax.axis_size(axis)
    place = lax.axis_index(axis)
    ahead = count - 1 - place if reverse else place
    gathered = jax.tree.map(lambda a: lax.all_gather(a, axis), part)
    state = jax.tree.map(lambda a, e: jnp.zeros_like(a) + jnp.asarray(e, a.dtype), part, identity)

    def one(lap, state):
        source = count - 1 - lap if reverse else lap
        return combine(
            state, jax.tree.map(lambda a: lax.dynamic_index_in_dim(a, source, 0, False), gathered)
        )

    return lax.fori_loop(0, ahead, one, state)


def layer_norm(rows_in, gain, shift):
    row_mean = jnp.mean(rows_in, axis=-1, keepdims=True)
    centred = rows_in - row_mean
    row_var = jnp.mean(centred * centred, axis=-1, keepdims=True)
    return centred * lax.rsqrt(row_var + EPSILON) * gain + shift


def silu_slope(pre_act):
    sigmoid_val = jax.nn.sigmoid(pre_act)
    return sigmoid_val * (1.0 + pre_act * (1.0 - sigmoid_val))


def segment_info(lengths, positions):
    first_end = lengths[0]
    second_end = lengths[0] + lengths[1]
    segment = (positions >= first_end).astype(jnp.int32) + (positions >= second_end).astype(
        jnp.int32
    )
    starts = ((positions == 0) | (positions == first_end) | (positions == second_end)).astype(
        jnp.float32
    )
    live_rows = (segment < 2).astype(jnp.float32)
    return (segment, starts, live_rows)


def combine_pair(earlier, following):
    return (earlier[0] * following[0], earlier[1] * following[0] + following[1])


def ema_local(normed, live_rows, starts, ema_rate, ema_damp, ema_in, ema_out, ema_skip, state_in):
    inputs = normed * live_rows[:, None]
    keep_rate = 1.0 - ema_rate * ema_damp
    drive_rate = ema_rate * ema_in
    decay = keep_rate[None] * (1.0 - starts)[:, None, None]
    drive = drive_rate[None] * inputs[:, None, :]
    decay_cum, partial_state = lax.associative_scan(combine_pair, (decay, drive), axis=0)
    states = partial_state + decay_cum * state_in[None]
    smooth = jnp.sum(states * ema_out[None], axis=1)
    ema_mixed = jax.nn.silu(smooth + ema_skip * normed)
    return (ema_mixed, states[-1])


def block_bias(rel_bias, bucket_map):
    by_offset = jnp.take(rel_bias, bucket_map)
    row_index = jnp.arange(BLOCK, dtype=jnp.int32)
    offsets = row_index[:, None] - row_index[None, :]
    return (jnp.take(by_offset, jnp.clip(offsets, 0, BLOCK - 1)), offsets)


def attention_probs(query_all, key_all, segment_all, bias_table, offsets):
    blocks = query_all.shape[0] // BLOCK
    query_blocks = query_all.reshape(blocks, BLOCK, -1)
    key_blocks = key_all.reshape(blocks, BLOCK, -1)
    seg_blocks = segment_all.reshape(blocks, BLOCK)
    allowed = (seg_blocks[:, :, None] == seg_blocks[:, None, :]) & (offsets >= 0)[None]
    score_scale = query_all.shape[-1] ** (-0.5)
    scores = (
        jnp.einsum("bik,bjk->bij", query_blocks, key_blocks, preferred_element_type=jnp.float32)
        * score_scale
    )
    scores = jnp.where(allowed, scores + bias_table[None], NEGATIVE)
    row_max = jnp.max(scores, axis=-1, keepdims=True)
    weighted = jnp.exp(scores - row_max)
    return weighted / jnp.sum(weighted, axis=-1, keepdims=True)


def shards(
    tokens,
    cotangent,
    seq_lengths,
    bucket_map,
    norm1_gain,
    norm1_bias,
    ema_rate,
    ema_damp,
    ema_in,
    ema_out,
    ema_skip,
    w_shared,
    qk_gain,
    qk_bias,
    rel_bias,
    w_value,
    w_reset,
    w_mix,
    w_hidden,
    w_update,
    b_update,
    norm2_gain,
    norm2_bias,
    w_up,
    b_up,
    w_down,
):
    row_count = tokens.shape[0]
    narrow_count = lax.axis_size("narrow")
    narrow_rank = lax.axis_index("narrow")
    group_rows = row_count * narrow_count
    blocks = group_rows // BLOCK
    local_blocks = row_count // BLOCK
    lengths = seq_lengths[0]
    local_positions = narrow_rank * row_count + jnp.arange(row_count, dtype=jnp.int32)
    segment_local, starts, live_rows = segment_info(lengths, local_positions)
    segment_all = segment_info(lengths, jnp.arange(group_rows, dtype=jnp.int32))[0]
    tokens_f = tokens.astype(jnp.float32)
    normed, norm1_back = jax.vjp(layer_norm, tokens_f, norm1_gain, norm1_bias)

    def ema_apply(normed_in, rate_in, damp_in, in_weight, out_weight, skip_in, state_in):
        return ema_local(
            normed_in, live_rows, starts, rate_in, damp_in, in_weight, out_weight, skip_in, state_in
        )

    zero_state = jnp.zeros_like(ema_rate)
    ones_state = jnp.ones_like(ema_rate)
    local_final = ema_apply(normed, ema_rate, ema_damp, ema_in, ema_out, ema_skip, zero_state)[1]
    through = jnp.power(1.0 - ema_rate * ema_damp, row_count) * (1.0 - jnp.max(starts))
    state_in = carried_in(
        (through, local_final), "narrow", combine_pair, (ones_state, zero_state), False
    )[1]
    (ema_mixed, final_state), ema_back = jax.vjp(
        ema_apply, normed, ema_rate, ema_damp, ema_in, ema_out, ema_skip, state_in
    )
    normed_low = normed.astype(jnp.bfloat16)
    mixed_low = ema_mixed.astype(jnp.bfloat16)
    pre_shared = jnp.dot(mixed_low, w_shared, preferred_element_type=jnp.float32)
    shared_act = jax.nn.silu(pre_shared)
    query_low = (shared_act * qk_gain[0] + qk_bias[0]).astype(jnp.bfloat16)
    key_low = (shared_act * qk_gain[1] + qk_bias[1]).astype(jnp.bfloat16)
    normed_all, mixed_all, query_all, key_all = (
        lax.all_gather(normed_low, "narrow", axis=0, tiled=True),
        lax.all_gather(mixed_low, "narrow", axis=0, tiled=True),
        lax.all_gather(query_low, "narrow", axis=0, tiled=True),
        lax.all_gather(key_low, "narrow", axis=0, tiled=True),
    )
    bias_table, offsets = block_bias(rel_bias, bucket_map)
    probs_low = attention_probs(query_all, key_all, segment_all, bias_table, offsets).astype(
        jnp.bfloat16
    )
    pre_value = jnp.dot(normed_all, w_value, preferred_element_type=jnp.float32)
    value_low = jax.nn.silu(pre_value).astype(jnp.bfloat16)
    value_blocks = value_low.reshape(blocks, BLOCK, -1)
    pre_reset = jnp.dot(mixed_all, w_reset, preferred_element_type=jnp.float32)
    reset_gate = jax.nn.silu(pre_reset)
    attended = jnp.einsum(
        "bij,bjv->biv", probs_low, value_blocks, preferred_element_type=jnp.float32
    ).reshape(group_rows, -1)
    gated_low = (reset_gate * attended).astype(jnp.bfloat16)
    piece = gated_low
    mix_part = lax.psum_scatter(
        jnp.dot(piece, w_mix, preferred_element_type=jnp.float32),
        "narrow",
        scatter_dimension=0,
        tiled=True,
    )
    pre_hidden = jnp.dot(mixed_low, w_hidden, preferred_element_type=jnp.float32) + mix_part
    hidden_act = jax.nn.silu(pre_hidden)
    pre_update = jnp.dot(mixed_low, w_update, preferred_element_type=jnp.float32) + b_update
    update_gate = jax.nn.sigmoid(pre_update)
    blended = update_gate * hidden_act + (1.0 - update_gate) * tokens_f
    normed2, norm2_back = jax.vjp(layer_norm, blended, norm2_gain, norm2_bias)
    normed2_low = normed2.astype(jnp.bfloat16)
    grad_out = cotangent.astype(jnp.float32) * live_rows[:, None]
    grad_out_low = grad_out.astype(jnp.bfloat16)
    normed2_all = lax.all_gather(normed2_low, "narrow", axis=0, tiled=True)
    pre_up = jnp.dot(normed2_all, w_up, preferred_element_type=jnp.float32) + b_up.astype(
        jnp.float32
    )
    up_low = jax.nn.silu(pre_up).astype(jnp.bfloat16)
    piece = up_low
    ffn_out = lax.psum_scatter(
        jnp.dot(piece, w_down, preferred_element_type=jnp.float32),
        "narrow",
        scatter_dimension=0,
        tiled=True,
    )
    grad_out_all = lax.all_gather(grad_out_low, "narrow", axis=0, tiled=True)
    grad_up = jnp.einsum("sd,fd->sf", grad_out_all, w_down, preferred_element_type=jnp.float32)
    grad_pre_up = (grad_up * silu_slope(pre_up)).astype(jnp.bfloat16)
    grad_w_down = jnp.einsum("sf,sd->fd", up_low, grad_out_all, preferred_element_type=jnp.float32)
    grad_w_up = jnp.einsum(
        "sd,sf->df", normed2_all, grad_pre_up, preferred_element_type=jnp.float32
    )
    grad_b_up = jnp.sum(grad_pre_up.astype(jnp.float32), axis=0)
    piece = grad_pre_up
    grad_normed2 = lax.psum_scatter(
        jnp.einsum("sf,df->sd", piece, w_up, preferred_element_type=jnp.float32),
        "narrow",
        scatter_dimension=0,
        tiled=True,
    )
    block_out = (blended + ffn_out).astype(jnp.bfloat16)
    grad_blended_norm, grad_norm2_gain, grad_norm2_bias = norm2_back(grad_normed2)
    grad_blended = grad_out + grad_blended_norm
    grad_hidden = grad_blended * update_gate
    grad_gate = grad_blended * (hidden_act - tokens_f)
    grad_tokens = grad_blended * (1.0 - update_gate)
    grad_pre_update = (grad_gate * update_gate * (1.0 - update_gate)).astype(jnp.bfloat16)
    grad_pre_hidden = (grad_hidden * silu_slope(pre_hidden)).astype(jnp.bfloat16)
    grad_b_update = jnp.sum(grad_pre_update.astype(jnp.float32), axis=0)
    grad_w_update = jnp.einsum(
        "sd,se->de", mixed_low, grad_pre_update, preferred_element_type=jnp.float32
    )
    grad_w_hidden = jnp.einsum(
        "sd,se->de", mixed_low, grad_pre_hidden, preferred_element_type=jnp.float32
    )
    hidden_all = lax.all_gather(grad_pre_hidden, "narrow", axis=0, tiled=True)
    grad_w_mix = jnp.einsum("sv,sd->vd", gated_low, hidden_all, preferred_element_type=jnp.float32)
    grad_gated = jnp.einsum("sd,vd->sv", hidden_all, w_mix, preferred_element_type=jnp.float32)
    grad_reset = grad_gated * attended
    grad_attended = (grad_gated * reset_gate).astype(jnp.bfloat16)
    grad_pre_reset = (grad_reset * silu_slope(pre_reset)).astype(jnp.bfloat16)
    grad_w_reset = jnp.einsum(
        "sd,sv->dv", mixed_all, grad_pre_reset, preferred_element_type=jnp.float32
    )
    attended_blocks = grad_attended.reshape(blocks, BLOCK, -1)
    probs_again = attention_probs(query_all, key_all, segment_all, bias_table, offsets)
    grad_probs = jnp.einsum(
        "biv,bjv->bij", attended_blocks, value_blocks, preferred_element_type=jnp.float32
    )
    grad_value = jnp.einsum(
        "bij,biv->bjv",
        probs_again.astype(jnp.bfloat16),
        attended_blocks,
        preferred_element_type=jnp.float32,
    ).reshape(group_rows, -1)
    grad_pre_value = (grad_value * silu_slope(pre_value)).astype(jnp.bfloat16)
    grad_w_value = jnp.einsum(
        "sd,sv->dv", normed_all, grad_pre_value, preferred_element_type=jnp.float32
    )
    mixed_cols = jnp.einsum(
        "sv,dv->sd", grad_pre_reset, w_reset, preferred_element_type=jnp.float32
    )
    normed_cols = jnp.einsum(
        "sv,dv->sd", grad_pre_value, w_value, preferred_element_type=jnp.float32
    )
    probs_rows, mixed_back, normed_back = (
        lax.psum_scatter(
            grad_probs.reshape(group_rows, BLOCK), "narrow", scatter_dimension=0, tiled=True
        ),
        lax.psum_scatter(mixed_cols, "narrow", scatter_dimension=0, tiled=True),
        lax.psum_scatter(normed_cols, "narrow", scatter_dimension=0, tiled=True),
    )
    probs_local = lax.dynamic_slice_in_dim(probs_again, narrow_rank * local_blocks, local_blocks, 0)
    grad_probs_local = probs_rows.reshape(local_blocks, BLOCK, BLOCK)
    grad_scores = probs_local * (
        grad_probs_local - jnp.sum(grad_probs_local * probs_local, axis=-1, keepdims=True)
    )
    grad_scores_low = grad_scores.astype(jnp.bfloat16)
    score_scale = query_low.shape[-1] ** (-0.5)
    query_blocks = query_low.reshape(local_blocks, BLOCK, -1)
    key_blocks = key_low.reshape(local_blocks, BLOCK, -1)
    grad_query = (
        jnp.einsum(
            "bij,bjk->bik", grad_scores_low, key_blocks, preferred_element_type=jnp.float32
        ).reshape(row_count, -1)
        * score_scale
    )
    grad_key = (
        jnp.einsum(
            "bij,bik->bjk", grad_scores_low, query_blocks, preferred_element_type=jnp.float32
        ).reshape(row_count, -1)
        * score_scale
    )
    score_total = jnp.sum(grad_scores_low.astype(jnp.float32), axis=0)
    offset_hits = (offsets[:, :, None] == jnp.arange(BLOCK, dtype=jnp.int32)[None, None, :]).astype(
        jnp.float32
    )
    grad_offset = jnp.sum(score_total[:, :, None] * offset_hits, axis=(0, 1))
    bucket_hits = (
        bucket_map[:, None] == jnp.arange(rel_bias.shape[0], dtype=jnp.int32)[None, :]
    ).astype(jnp.float32)
    grad_rel_bias = jnp.sum(grad_offset[:, None] * bucket_hits, axis=0)
    grad_shared_act = grad_query * qk_gain[0] + grad_key * qk_gain[1]
    grad_qk_gain = jnp.stack(
        [jnp.sum(grad_query * shared_act, axis=0), jnp.sum(grad_key * shared_act, axis=0)]
    )
    grad_qk_bias = jnp.stack([jnp.sum(grad_query, axis=0), jnp.sum(grad_key, axis=0)])
    grad_pre_shared = (grad_shared_act * silu_slope(pre_shared)).astype(jnp.bfloat16)
    grad_w_shared = jnp.einsum(
        "sd,sz->dz", mixed_low, grad_pre_shared, preferred_element_type=jnp.float32
    )
    grad_mixed = (
        mixed_back
        + jnp.einsum("sz,dz->sd", grad_pre_shared, w_shared, preferred_element_type=jnp.float32)
        + jnp.einsum("se,de->sd", grad_pre_hidden, w_hidden, preferred_element_type=jnp.float32)
        + jnp.einsum("se,de->sd", grad_pre_update, w_update, preferred_element_type=jnp.float32)
    )
    direct = ema_back((grad_mixed, zero_state))
    later_state = carried_in(
        (through, direct[6]), "narrow", combine_pair, (ones_state, zero_state), True
    )[1]
    chained = ema_back((jnp.zeros_like(ema_mixed), later_state))
    grad_normed = normed_back + direct[0] + chained[0]
    grad_tokens_norm, grad_norm1_gain, grad_norm1_bias = norm1_back(grad_normed)
    grad_tokens = grad_tokens + grad_tokens_norm
    grad_ema_rate = direct[1] + chained[1]
    grad_ema_damp = direct[2] + chained[2]
    grad_ema_in = direct[3] + chained[3]
    grad_ema_out = direct[4] + chained[4]
    grad_ema_skip = direct[5] + chained[5]
    grad_w_value, grad_w_reset, grad_w_mix, grad_w_up, grad_b_up, grad_w_down = lax.psum(
        (grad_w_value, grad_w_reset, grad_w_mix, grad_w_up, grad_b_up, grad_w_down), "wide"
    )
    (
        grad_norm1_gain,
        grad_norm1_bias,
        grad_ema_rate,
        grad_ema_damp,
        grad_ema_in,
        grad_ema_out,
        grad_ema_skip,
        grad_w_shared,
        grad_qk_gain,
        grad_qk_bias,
        grad_rel_bias,
        grad_w_hidden,
        grad_w_update,
        grad_b_update,
        grad_norm2_gain,
        grad_norm2_bias,
    ) = lax.psum(
        (
            grad_norm1_gain,
            grad_norm1_bias,
            grad_ema_rate,
            grad_ema_damp,
            grad_ema_in,
            grad_ema_out,
            grad_ema_skip,
            grad_w_shared,
            grad_qk_gain,
            grad_qk_bias,
            grad_rel_bias,
            grad_w_hidden,
            grad_w_update,
            grad_b_update,
            grad_norm2_gain,
            grad_norm2_bias,
        ),
        ("wide", "narrow"),
    )
    return (
        block_out,
        grad_tokens,
        grad_norm1_gain,
        grad_norm1_bias,
        grad_ema_rate,
        grad_ema_damp,
        grad_ema_in,
        grad_ema_out,
        grad_ema_skip,
        grad_w_shared,
        grad_qk_gain,
        grad_qk_bias,
        grad_rel_bias,
        grad_w_value,
        grad_w_reset,
        grad_w_mix,
        grad_w_hidden,
        grad_w_update,
        grad_b_update,
        grad_norm2_gain,
        grad_norm2_bias,
        grad_w_up,
        grad_b_up,
        grad_w_down,
    )


NZ = 4
ROOT = 1
NEAR = (0, 2, 3)
EVEN, ENDS = (0, 1, 2, 3), (0, 3, 0, 3)
MIXED = (0, 3, 1, 2)
UNITS = (
    (0, 1, 0, 512, ENDS), (0, 0, 512, 512, MIXED), (1, 2, 0, 512, EVEN), (1, 0, 512, 512, ENDS), (2, 0, 0, 256, ENDS), (2, 1, 256, 768, ENDS),
    (3, 1, 0, 768, EVEN), (3, 1, 768, 256, MIXED), (4, 1, 0, 768, ENDS), (4, 1, 768, 256, ENDS), (5, 2, 0, 512, EVEN), (5, 0, 512, 512, EVEN),
    (6, 2, 0, 256, ENDS), (6, 2, 256, 768, ENDS), (7, 1, 0, 512, ENDS), (7, 1, 512, 512, ENDS),
)
PHASES = (1.5, 1.0, 2.0, 1.5, 3.5, 1.2, 5.5, 1.5, 1.5, 1.5, 1.0, 1.0, 0.8, 1.5, 0.8, 2.0, 0.8, 1.0, 2.0, 1.3, 1.3, 1.3, 1.3, 4.0, 1.0)
RELEASE = {0: 0, 1: 0, 2: 3, 3: 3, 4: 12, 5: 14, 6: 16, 7: 17}
EARLY = tuple(u for u, t in enumerate(UNITS) if t[0] < 2)
UNIT, LAG = 3.0, 2.0
MARGIN, WINDOW = 0.0, 1000.0
RANKS = {"G": 1, "P": 1, "C": 1, "D": 1, "F": 1, "W": 1, "Y": 4, "X": 4, "S": 0}
BY_UNIT = False


def far_first(z, roots):
    return sorted(range(NZ), key=lambda k: (-abs(roots[k] - z), k))


def line_events(z):
    found = []
    for u, (i, first, _, rows, roots) in enumerate(UNITS):
        size = rows / (1024.0 if first else 512.0)
        late = RELEASE[i]
        for k in range(NZ):
            g = roots[k]
            left = ("l", z - 1, ("zr", u, k), size)
            right = ("r", z + 1, ("zl", u, k), size)
            cross = [("y", z, ("yf", u, k), size)]
            far = [("x", z, ("xf", u, k, 0), size)] if i == 5 else []
            far += [("c", z, ("cf", u, k, 0), size)]
            on = (cross if first == 1 else []) + far
            both = ([left] if z > 0 else []) + ([right] if z < NZ - 1 else []) + (cross if first else []) + far
            need = [("yr", u, k)] if first else []
            if first:
                found.append((("G", u, k), late, None, [], [("y", z, ("yr", u, k), size)], 0.1))
            if z > 0 and g >= z:
                need.append(("zl", u, k))
            if z < NZ - 1 and g <= z:
                need.append(("zr", u, k))
            if g != z:
                found.append((("P", u, k), late, None, need, [right if g > z else left], 0.4))
                further = [left] if g > z > 0 else [right] if g < z < NZ - 1 else []
                found.append((("F", u, k), late, ("P", u, k), [("zr" if g > z else "zl", u, k)], further + on, 0.2))
            else:
                swap = both if first else [("y", z, ("yr", u, k), size)]
                found.append((("C", u, k), late, None, need, swap, 0.4))
                if not first:
                    found.append((("D", u, k), late, ("C", u, k), [("yr", u, k)], both, 0.4))
            other = [("x", z, ("xf", u, k, 1), size)] if i == 5 else []
            other += [("c", z, ("cf", u, k, 1), size)]
            if first == 1:
                found.append((("Y", u, k), late, ("G", u, k), [("yf", u, k)], other, 0.2))
            if first == 2:
                left = ("l", z - 1, ("wr", u, k), size)
                right = ("r", z + 1, ("wl", u, k), size)
                if g == z:
                    both = ([left] if z > 0 else []) + ([right] if z < NZ - 1 else []) + other
                    found.append((("Y", u, k), late, ("G", u, k), [("yf", u, k)], both, 0.2))
                else:
                    further = [left] if g > z > 0 else [right] if g < z < NZ - 1 else []
                    found.append((("W", u, k), late, ("G", u, k), [("wr" if g > z else "wl", u, k)], further + other, 0.2))
            if i == 5:
                for h in range(2 if first else 1):
                    found.append((("X", u, k, h), late, None, [("xf", u, k, h)], [("c", z, ("cf", u, k, 2 + h), size)], 0.2))
    last = len(PHASES) - 1

    def small(n, after, need, out):
        found.append((("S", n, 0), last, after, need, out, 0.4))

    small(1, None, [], [("x", z, ("s1",), 0.7), ("c", z, ("s1c",), 0.7)])
    small(3, ("S", 1, 0), [("s1",)], [("y", z, ("s3",), 1.35)])
    inward = [] if z == ROOT else [("r" if z < ROOT else "l", ROOT, ("s4", z), 1.35)]
    small(4, ("S", 3, 0), [("s3",)], inward)
    tail = [("c", z, ("s6",), 1.35), ("x", z, ("s7",), 1.35)]
    if z == ROOT:
        out = [("l" if q < ROOT else "r", q, ("s5",), 1.35) for q in NEAR]
        small(6, ("S", 4, 0), [("s4", q) for q in NEAR], out + tail)
    else:
        small(7, ("S", 4, 0), [("s5",)], tail)
    return found


def make_plan():
    todo = [line_events(z) for z in range(NZ)]
    clock = [0.0] * NZ
    phase = [0] * NZ
    done = [set() for _ in range(NZ)]
    arrive = [{} for _ in range(NZ)]
    link = {}
    plan = [[[] for _ in range(len(PHASES) + 1)] for _ in range(NZ)]
    while any(todo) or min(phase) < len(PHASES):
        z = min(range(NZ), key=lambda q: (clock[q], q) if (todo[q] or phase[q] < len(PHASES)) else (1e9, q))
        now = clock[z]
        best = None
        for item in todo[z]:
            key, late, after, need, out, cost = item
            if phase[z] <= late or (after is not None and after not in done[z]):
                continue
            latest = 0.0
            for m in need:
                latest = max(latest, arrive[z].get(m, 1e9))
            if need and latest + (MARGIN if phase[z] < len(PHASES) else 0.0) > now:
                continue
            full = phase[z] >= len(PHASES) and key[0] != "S" and any(
                link.get((z, lane), 0.0) > now + WINDOW for lane, _, _, _ in out if lane in "ylr")
            if full:
                continue
            away = -abs(UNITS[key[1]][4][key[2]] - z) if key[0] != "S" else 0
            rank = RANKS[key[0]]
            if key[0] == "Y" and UNITS[key[1]][1] == 2:
                rank = RANKS["F"]
            order = (rank, key[1] if BY_UNIT else latest, away, key[1], key[2])
            if best is None or order < best[0]:
                best = (order, item)
        if best is not None:
            item = best[1]
            todo[z].remove(item)
            key, _, _, _, out, cost = item
            done[z].add(key)
            plan[z][phase[z]].append(key)
            clock[z] += cost
            for lane, dest, message, size in out:
                begin = max(link.get((z, lane), 0.0), clock[z])
                took = size * UNIT * (0.2 if lane == "c" else 1.0)
                link[(z, lane)] = begin + took
                arrive[dest][message] = begin + took + LAG
        elif phase[z] < len(PHASES):
            clock[z] += PHASES[phase[z]]
            phase[z] += 1
        else:
            clock[z] += 0.1
    ends = [max([clock[z]] + list(arrive[z].values())) for z in range(NZ)]
    return plan, ends

F32 = jnp.float32
BF = jnp.bfloat16
MESH = pl.DeviceIdType.MESH


def mm(a, b):
    return lax.dot_general(a, b, (((1,), (0,)), ((), ())), preferred_element_type=F32)


def mm_nt(a, b):
    return lax.dot_general(a, b, (((1,), (1,)), ((), ())), preferred_element_type=F32)


def mm_tn(a, b):
    return lax.dot_general(a, b, (((0,), (0,)), ((), ())), preferred_element_type=F32)


def sigm(v):
    return 1.0 / (1.0 + jnp.exp(-v))


def slope_of(pre, sig):
    return sig * (1.0 + pre * (1.0 - sig))


def cols(i, n):
    return pl.ds(pl.multiple_of(i * n, n), n)


def main_kernel(
    tok_h, cot_h, wsh_h, wv_h, wr_h, wm_h, wh_h, wu_h, wup_h, wdn_h,
    lens, relb, bmap, in_n1g, in_n1b, in_skip, in_bupd, in_n2g, in_n2b, rate, damp, ein, eout, qkg, qkb, in_bup,
    bo, gt, o_down, o_up, o_mix, o_hu, o_reset, o_value, o_shared, o_small,
    wsh, wv, wr, wm, wh, wu, wup, wdn,
    tok, gout, normed, nlow, mlow, pre_ema, xs, smo, pre_sh, qlow, klow, probs, plow,
    pre_v, att, pre_r, vlow, gated, part_s, mix_r, own_f, pre_hid, gate, blend, n2,
    gup, up, gpu, gn2_r, ffn_s, ffn_r, hid, upd, gpr, gpv, gp_acc, gp_r, gps,
    nb_s, mb_r, nb_r,
    p_normed, p_mixed, p_gout, p_up, p_n2, p_gpu, p_gated, p_hid, p_upd, p_gpr, p_gpv, p_gps,
    a_s, w_s, snap_s, snap_r, carry, carry_r, acc, keep, live, segc, vec, bup,
    g_v, ext, small, s_q, s_own, s_y, s_in,
    wsem, xsend, xrecv, csend, crecv, lsem, asend, arecv, ready,
):
    x = lax.axis_index("narrow")
    w = lax.axis_index("wide")
    other = 1 - x
    c = w % 2
    wpart = w + 1 - 2 * c
    y = (w // 2) % 2
    wy = w + 2 - 4 * y
    zi = w // 4
    wl = w - 4
    wr_ = w + 4
    H = tok.shape[0] // 2
    R = 2 * H
    own = pl.ds(pl.multiple_of(x * H, H), H)
    oth = pl.ds(pl.multiple_of(other * H, H), H)
    D = 1024
    VL = wv.shape[1]
    FL = wup.shape[1]
    EPS = EPSILON

    weights = [
        (tok_h, tok.at[own]), (cot_h, gout.at[own]), (wsh_h, wsh), (wv_h, wv), (wr_h, wr), (wm_h, wm), (wh_h, wh), (wu_h, wu), (wdn_h, wdn),
        (wup_h, wup),
    ]
    wcopies = [pltpu.make_async_copy(s, d, wsem.at[i]) for i, (s, d) in enumerate(weights)]
    wcopies[0].start()
    wcopies[1].start()

    barrier = pltpu.get_barrier_semaphore()
    w_root = w + 4 * (ROOT - zi)
    w_last = w + 4 * (NZ - 1 - zi)

    def greet(to):
        pl.semaphore_signal(barrier, inc=1, device_id=to, device_id_type=MESH)

    for to in ((w, other), (wpart, x), (wpart, other), (wy, x)):
        greet(to)
    for z in range(NZ):
        met = [wl] * (z > 0) + [wr_] * (z < NZ - 1) + [w_last] * (z == ROOT) + [w_root] * (z == NZ - 1)

        @pl.when(zi == z)
        def _(met=met):
            for to in met:
                greet((to, x))
            pl.semaphore_wait(barrier, 4 + len(met))

    def xcopy(i, src, dst):
        return pltpu.make_async_remote_copy(
            src_ref=src, dst_ref=dst, send_sem=xsend.at[i], recv_sem=xrecv.at[i],
            device_id=(w, other), device_id_type=MESH,
        )

    def ccopy(i, src, dst):
        return pltpu.make_async_remote_copy(
            src_ref=src, dst_ref=dst, send_sem=csend.at[i], recv_sem=crecv.at[i],
            device_id=(wpart, x), device_id_type=MESH,
        )

    HC = H // 4
    x_tok = [
        xcopy(0 if j == 0 else 16 + j, tok_h.at[j * HC : (j + 1) * HC], tok.at[pl.ds(pl.multiple_of(x * H + j * HC, HC), HC)])
        for j in range(4)
    ]
    x_cot = xcopy(1, cot_h, gout.at[own])
    for copy in x_tok:
        copy.start()
    for copy in wcopies[2:]:
        copy.start()

    gs = smo.at[0 : H * 8]
    gxs = smo.at[H * 8 : R * 8]
    nb_o = gup.at[0:H, 0:D]
    gres = gup.at[0:H, D : 2 * D]
    ffn_o = gup.at[H:R, 0:D]

    first_end = lens[0, 0]
    second_end = first_end + lens[0, 1]
    place = lax.broadcasted_iota(jnp.int32, (R, 128), 0)
    begins = (place == 0) | (place == first_end) | (place == second_end)
    keep[...] = jnp.where(begins, 0.0, 1.0)
    live[...] = jnp.where(place >= second_end, 0.0, 1.0)

    def segment_of(at):
        return jnp.where(at >= first_end, 1.0, 0.0) + jnp.where(at >= second_end, 1.0, 0.0)

    segc[...] = segment_of(place)

    for t in range(2):
        for j in range(8):
            rows_ = slice(t * 8, t * 8 + 8)
            lanes = slice(j * 128, j * 128 + 128)
            r_ = rate[rows_, lanes]
            a_s[pl.ds(t * 64 + j, 8, stride=8), :] = 1.0 - r_ * damp[rows_, lanes]
            w_s[pl.ds(t * 64 + j, 8, stride=8), :] = r_ * ein[rows_, lanes] * eout[rows_, lanes]

    for k, ref in enumerate((in_n1g, in_n1b, in_skip, in_bupd, in_n2g, in_n2b)):
        for j in range(8):
            vec[k : k + 1, j * 128 : (j + 1) * 128] = ref[j : j + 1, :]
    wide_bias = in_bup[...].astype(F32)
    for j in range(16):
        bup[0:1, j * 128 : (j + 1) * 128] = wide_bias[j : j + 1, :]

    def norm_rows(v):
        m = jnp.mean(v, axis=-1, keepdims=True)
        cen = v - m
        var = jnp.mean(cen * cen, axis=-1, keepdims=True)
        return cen, lax.rsqrt(var + EPS)

    def norm1(t):
        rr = cols(t, 16)
        cen, rstd = norm_rows(tok[rr, :].astype(F32))
        v = cen * rstd * vec[0:1, :] + vec[1:2, :]
        normed[rr, :] = v
        nlow[rr, :] = v.astype(BF)
        for j in range(8):
            xs[pl.ds(t * 128 + j, 16, stride=8), :] = v[:, j * 128 : (j + 1) * 128]

    HT = H // 16
    wcopies[0].wait()
    pl.loop(0, HT)(lambda t: norm1(x * HT + t))
    N = 16

    def coef(ref):
        return ref[...].reshape(N, 8, 128)

    zeros = jnp.zeros((N, 8, 128), F32)

    def forward(p, s):
        k = keep[pl.ds(p, 1), :]
        at = cols(p, 8)
        xr = xs[at, :] * live[pl.ds(p, 1), :]
        s = coef(a_s) * (s * k) + xr
        smo[at, :] = jnp.sum(coef(w_s) * s, axis=0)
        return s

    def mixed_rows(t):
        rr = cols(t, 16)
        for j in range(8):
            ll = slice(j * 128, (j + 1) * 128)
            pre = smo[pl.ds(t * 128 + j, 16, stride=8), :] + vec[2:3, ll] * normed[rr, ll]
            pre_ema[rr, ll] = pre
            mlow[rr, ll] = (pre * sigm(pre)).astype(BF)

    T = 256

    def value_tile(i, rows_):
        cc = cols(i, T)
        pv = mm(nlow[rows_, :], wv[:, cc])
        pre_v[rows_, cc] = pv
        vlow[rows_, cc] = (pv * sigm(pv)).astype(BF)

    wcopies[3].wait()
    pl.loop(0, VL // T, unroll=2)(lambda i: value_tile(i, own))
    state = zeros
    for j in range(8):

        @pl.when(x == (1 if j < 4 else 0))
        def _(j=j):
            x_tok[j % 4].wait_recv()
            pl.loop(j * (HC // 16), (j + 1) * (HC // 16))(norm1)

        state = lax.fori_loop(j * HC, (j + 1) * HC, forward, state, unroll=4)
        pl.loop(j * (HC // 16), (j + 1) * (HC // 16))(mixed_rows)

    for copy in x_tok:
        copy.wait_send()
    x_cot.start()
    c_normed = ccopy(0, nlow, p_normed)
    c_normed.start()
    c_mixed = ccopy(1, mlow, p_mixed)
    c_mixed.start()

    wcopies[2].wait()
    psh = mm(mlow[...], wsh[...])
    pre_sh[...] = psh
    sh = psh * sigm(psh)
    qlow[...] = (sh * qkg[0:1, :] + qkb[0:1, :]).astype(BF)
    klow[...] = (sh * qkg[1:2, :] + qkb[1:2, :]).astype(BF)

    BL = BLOCK
    ii = lax.broadcasted_iota(jnp.int32, (BL, BL), 0)
    jj = lax.broadcasted_iota(jnp.int32, (BL, BL), 1)

    def skew(tbl, left):
        for b in range(7):
            moved = pltpu.roll(tbl, (BL - (1 << b)) if left else (1 << b), 1)
            tbl = jnp.where(lax.rem(ii // (1 << b), 2) == 1, moved, tbl)
        return tbl

    buckets = bmap[0:1, :]
    by_offset = jnp.zeros((1, BL), F32)
    for b in range(relb.shape[1]):
        by_offset = by_offset + jnp.where(buckets == b, relb[0, b], 0.0)
    table = skew(jnp.broadcast_to(by_offset, (BL, BL)), False).T
    scale = float(qkg.shape[1]) ** (-0.5)
    for b in range(2):
        rb = slice(b * BL, (b + 1) * BL)
        sc = mm_nt(qlow[rb, :], klow[rb, :]) * scale
        ok = (segc[rb, :] == segment_of(lax.broadcasted_iota(jnp.int32, (1, BL), 1) + b * BL)) & (jj <= ii)
        sc = jnp.where(ok, sc + table, NEGATIVE)
        ex = jnp.exp(sc - jnp.max(sc, axis=-1, keepdims=True))
        pr = ex / jnp.sum(ex, axis=-1, keepdims=True)
        probs[rb, :] = pr
        plow[rb, :] = pr.astype(BF)

    wcopies[4].wait()

    def reset_tile(i):
        cc = cols(i, T)
        for b in range(2):
            rb = slice(b * BL, (b + 1) * BL)
            att[rb, cc] = mm(plow[rb, :], vlow[rb, cc])
        pr = mm(mlow[...], wr[:, cc])
        pre_r[:, cc] = pr
        gated[:, cc] = (pr * sigm(pr) * att[:, cc]).astype(BF)

    pl.loop(0, VL // T, unroll=2)(lambda i: value_tile(i, oth))
    pl.loop(0, VL // T, unroll=2)(reset_tile)

    wcopies[5].wait()

    HH = H // 2
    x_mix = []
    for h in range(2):
        src = pl.ds(pl.multiple_of(other * H + h * HH, HH), HH)
        hr = slice(h * HH, (h + 1) * HH)

        @pl.loop(0, D // T, unroll=2)
        def _(i, src=src, hr=hr):
            cc = cols(i, T)
            part_s[hr, cc] = mm(gated[src, :], wm[:, cc]).astype(BF)

        x_mix.append(xcopy((2, 13)[h], part_s.at[hr], mix_r.at[hr]))
        x_mix[h].start()

    c_gated = ccopy(2, gated, p_gated)
    c_gated.start()
    wcopies[6].wait()
    wcopies[7].wait()

    @pl.loop(0, D // T, unroll=2)
    def _(i):
        cc = cols(i, T)
        own_f[:, cc] = mm(gated[own, :], wm[:, cc])
        pre_hid[:, cc] = mm(mlow[own, :], wh[:, cc])
        gate[:, cc] = sigm(mm(mlow[own, :], wu[:, cc]) + vec[3:4, cc])

    wcopies[1].wait()
    x_cot.wait()

    @pl.loop(0, R // 16)
    def _(t):
        rr = cols(t, 16)
        gout[rr, :] = (gout[rr, :].astype(F32) * live[rr, 0:1]).astype(BF)

    c_gout = ccopy(3, gout, p_gout)
    c_gout.start()
    wcopies[8].wait()

    @pl.loop(0, FL // T, unroll=2)
    def _(i):
        cc = cols(i, T)
        gup[:, cc] = mm_nt(gout[...], wdn[cc, :])


    def blend_rows(t):
        rr = cols(t, 16)
        ro = pl.ds(pl.multiple_of(x * H + t * 16, 16), 16)
        ph = pre_hid[rr, :] + (own_f[rr, :] + mix_r[rr, :].astype(F32))
        pre_hid[rr, :] = ph
        u = gate[rr, :]
        bl = u * (ph * sigm(ph)) + (1.0 - u) * tok[ro, :].astype(F32)
        blend[rr, :] = bl
        cen, rstd = norm_rows(bl)
        n2[ro, :] = (cen * rstd * vec[4:5, :] + vec[5:6, :]).astype(BF)

    x_n2 = []
    for h in range(4):
        if h % 2 == 0:
            x_mix[h // 2].wait()
        pl.loop(h * (HT // 4), (h + 1) * (HT // 4))(blend_rows)
        part = pl.ds(pl.multiple_of(x * H + h * (H // 4), H // 4), H // 4)
        x_n2.append(xcopy(3 if h == 0 else 13 + h, n2.at[part], n2.at[part]))
        x_n2[h].start()

    wcopies[9].wait()
    FT = FL // T

    def up_tile(i, rows_, first):
        cc = cols(i, T)
        pu = mm(n2[rows_, :], wup[:, cc]) + bup[0:1, cc]
        sg = sigm(pu)
        up[rows_, cc] = (pu * sg).astype(BF)
        gp = (gup[rows_, cc] * slope_of(pu, sg)).astype(BF)
        gpu[rows_, cc] = gp
        sums = jnp.sum(gp.astype(F32), axis=0, keepdims=True)
        for h in range(2):
            at = pl.ds(304 + x * 16 + i * 2 + h, 1)
            part = sums[:, h * 128 : (h + 1) * 128]
            if first:
                small[at, :] = part
                small[pl.ds(304 + other * 16 + i * 2 + h, 1), :] = jnp.zeros((1, 128), F32)
            else:
                small[at, :] += part

    pl.loop(0, FT, unroll=2)(lambda i: up_tile(i, own, True))
    for copy in x_n2:
        copy.wait()
    c_n2 = ccopy(4, n2, p_n2)
    c_n2.start()
    halfF = FL // 2
    theirs_f = pl.ds(pl.multiple_of((1 - c) * halfF, halfF), halfF)
    pl.loop(0, FT // 2, unroll=2)(lambda i: up_tile((1 - c) * (FT // 2) + i, oth, False))
    c_up = ccopy(5, up.at[:, theirs_f], p_up)
    c_gpu = ccopy(6, gpu.at[:, theirs_f], p_gpu)
    c_up.start()
    c_gpu.start()
    pl.loop(0, FT // 2, unroll=2)(lambda i: up_tile(c * (FT // 2) + i, oth, False))
    P2 = g_v.shape[2]
    plan = make_plan()[0]
    numbers = {}
    locals_ = {}

    def number(*key):
        return numbers.setdefault(key, len(numbers))

    shelves = [[wup, 0, j, 0] for j in range(wup.shape[1] // P2)]
    shelves += [[wdn, 0, j, 0] for j in range(wdn.shape[1] // P2)] + [[ext, 0, 0, 0]]
    places = {}

    def place_of(key, n):
        if key not in places:
            for shelf in shelves:
                if (shelf[0] is ext) == (key[0] in EARLY) and shelf[1] + n <= shelf[0].shape[0]:
                    places[key] = (shelf[0], shelf[1], shelf[2] * P2)
                    shelf[1] += n
                    break
        ref, r0, c0 = places[key]
        return ref.at[r0 : r0 + n, c0 : c0 + P2]

    def chunk_rows(u):
        _, first, _, rows, _ = UNITS[u]
        return rows // 8 if first else rows // 4

    def earlier(u, k):
        roots = UNITS[u][4]
        return sum(roots[q] == roots[k] for q in range(k))

    def line_place(u, k):
        return place_of((u, "z", k), chunk_rows(u))

    def second_place(u, k):
        return place_of((u, "s", earlier(u, k)), chunk_rows(u))

    def cross_place(u, k):
        return place_of((u, "y", k if UNITS[u][1] else earlier(u, k)), chunk_rows(u))

    def from_right(u, k, z):
        return second_place(u, k) if UNITS[u][4][k] == z and z > 0 else line_place(u, k)

    def first_row(u, k, half):
        _, first, row0, rows, _ = UNITS[u]
        n = chunk_rows(u)
        if first:
            return row0 + half * (rows // 2) + k * n
        return row0 + k * n

    def rows_at(u, k, half):
        n = chunk_rows(u)
        if UNITS[u][1]:
            return pl.ds(pl.multiple_of(first_row(u, k, half), 16), n)
        return pl.ds(first_row(u, k, half), n)

    def chunk(u, k, half):
        return g_v.at[UNITS[u][0], rows_at(u, k, half)]

    def result(u, k, half, core, side):
        i = UNITS[u][0]
        n = chunk_rows(u)
        r0 = first_row(u, k, half)
        j = i % 2
        if i < 2:
            return o_down.at[pl.ds(pl.multiple_of(core * D + r0, 16), n), j * P2 : (j + 1) * P2]
        rr = pl.ds(pl.multiple_of(r0, 16), n)
        if i < 4:
            return o_up.at[rr, pl.ds(pl.multiple_of(core * D + j * P2, P2), P2)]
        if i == 5:
            return o_hu.at[2 * side + core, rr]
        ref = {4: o_mix, 6: o_reset, 7: o_value}[i]
        return ref.at[rr, pl.ds(pl.multiple_of(core * P2, P2), P2)]

    sent = [[] for _ in range(NZ)]

    def send(z, way, key, src, dst):
        dev = {
            "y": (wy, x), "l": (wl, x), "r": (wr_, x), "c": (wpart, x), "x": (w, other), "d": (wpart, other),
            "root": (w_root, x), "last": (w_last, x),
        }[way]
        n = number(*key)
        copy = pltpu.make_async_remote_copy(
            src_ref=src, dst_ref=dst, send_sem=asend.at[n], recv_sem=arecv.at[n],
            device_id=dev, device_id_type=MESH,
        )
        copy.start()
        sent[z].append((n, src.shape, src.dtype))

    def arrived(key, ref):
        n = number(*key)
        pltpu.make_async_remote_copy(
            src_ref=ref, dst_ref=ref, send_sem=asend.at[n], recv_sem=arecv.at[n],
            device_id=(w, other), device_id_type=MESH,
        ).wait_recv()

    def add_up(dst, terms):
        if terms:

            @pl.loop(0, dst.shape[0] // 32)
            def _(t):
                rr = cols(t, 32)
                v = dst[rr, :].astype(F32)
                for term in terms:
                    v = v + term[rr, :].astype(F32)
                dst[rr, :] = v.astype(BF)

    def own_copy(u, k, src, half):
        at = locals_.setdefault((u, k), len(locals_))
        return pltpu.make_async_copy(src, result(u, k, half, c, x), lsem.at[at])

    def share(z, u, k, src, half):
        dst = result(u, k, half, c, x)
        if z > 0:
            send(z, "l", ("zr", u, k), src, dst)
        if z < NZ - 1:
            send(z, "r", ("zl", u, k), src, dst)
        if UNITS[u][1]:
            send(z, "y", ("yf", u, k), src, dst)
        if UNITS[u][0] == 5:
            send(z, "x", ("xf", u, k, 0), src, dst)
        send(z, "c", ("cf", u, k, 0), src, dst)
        own_copy(u, k, src, half).start()

    def happen(z, key):
        kind, u, k = key[:3]
        if kind == "S":
            small_step(z, u)
            return
        i, first, _, _, roots = UNITS[u]
        own_half = y if first else 0
        g = roots[k]
        if kind == "G":
            send(z, "y", ("yr", u, k), chunk(u, k, 1 - y), cross_place(u, k))
            return
        if kind in "PC":
            terms = []
            if first:
                arrived(("yr", u, k), cross_place(u, k))
                terms.append(cross_place(u, k))
            if g >= z and z > 0:
                arrived(("zl", u, k), line_place(u, k))
                terms.append(line_place(u, k))
            if g <= z and z < NZ - 1:
                arrived(("zr", u, k), from_right(u, k, z))
                terms.append(from_right(u, k, z))
            mine = chunk(u, k, own_half)
            add_up(mine, terms)
            if kind == "P" and g > z:
                send(z, "r", ("zl", u, k), mine, line_place(u, k))
            elif kind == "P":
                send(z, "l", ("zr", u, k), mine, from_right(u, k, z - 1))
            elif first:
                share(z, u, k, mine, own_half)
            else:
                send(z, "y", ("yr", u, k), mine, cross_place(u, k))
        elif kind == "D":
            mine = cross_place(u, k)
            arrived(("yr", u, k), mine)
            add_up(mine, [chunk(u, k, 0)])
            share(z, u, k, mine, 0)
        elif kind == "F":
            ref = result(u, k, own_half, c, x)
            arrived(("zr" if g > z else "zl", u, k), ref)
            if g > z > 0:
                send(z, "l", ("zr", u, k), ref, ref)
            if g < z < NZ - 1:
                send(z, "r", ("zl", u, k), ref, ref)
            if first == 1:
                send(z, "y", ("yf", u, k), ref, ref)
            if i == 5:
                send(z, "x", ("xf", u, k, 0), ref, ref)
            send(z, "c", ("cf", u, k, 0), ref, ref)
        elif kind in "YW":
            ref = result(u, k, 1 - y, c, x)
            arrived(("yf" if kind == "Y" else "wr" if g > z else "wl", u, k), ref)
            if first == 2 and g >= z > 0:
                send(z, "l", ("wr", u, k), ref, ref)
            if first == 2 and g <= z < NZ - 1:
                send(z, "r", ("wl", u, k), ref, ref)
            if i == 5:
                send(z, "x", ("xf", u, k, 1), ref, ref)
            send(z, "c", ("cf", u, k, 1), ref, ref)
        elif kind == "X":
            h = key[3]
            half = (y if h == 0 else 1 - y) if first else 0
            ref = result(u, k, half, c, other)
            arrived(("xf", u, k, h), ref)
            send(z, "c", ("cf", u, k, 2 + h), ref, ref)

    def slot(n):
        for z in range(NZ):
            if plan[z][n]:

                @pl.when(zi == z)
                def _(z=z):
                    for key in plan[z][n]:
                        happen(z, key)

    def eight(start, n):
        return pl.ds(pl.multiple_of(start, 8), n)

    def quarter(side, core):
        return eight(side * 176 + core * 88, 88)

    def quarter_sh(side, core):
        return eight((2 * side + core) * 256, 256)

    around = (("x", other, c), ("c", x, 1 - c), ("d", other, 1 - c))

    def small_step(z, n):
        mine, mine_sh = quarter(x, c), quarter_sh(x, c)

        def give(total):
            o_small[mine, :] = total[0:88, :]
            o_shared[mine_sh, :] = total[88:344, :]
            for way, _, _ in around:
                send(z, way, ("s6", way), o_small.at[mine], o_small.at[mine])
                send(z, way, ("s7", way), o_shared.at[mine_sh], o_shared.at[mine_sh])

        if n == 1:
            for at, (way, side, core) in enumerate(around):
                send(z, way, ("s1", way), small.at[quarter(side, core)], s_q.at[at])
        elif n == 3:
            for at, (way, _, _) in enumerate(around):
                arrived(("s1", way), s_q.at[at])
            s_own[0:88, :] = (small[mine, :] + s_q[0]) + (s_q[1] + s_q[2])
            send(z, "y", ("s3",), s_own, s_y)
        elif n == 4:
            arrived(("s3",), s_y)
            s_y[...] = s_y[...] + s_own[...]
            if z != ROOT:
                send(z, "root", ("s4", z), s_y, s_in.at[NEAR.index(z)])
        elif n == 6:
            for at, q in enumerate(NEAR):
                arrived(("s4", q), s_in.at[at])
            s_y[...] = (s_y[...] + s_in[0]) + (s_in[1] + s_in[2])
            for q, way in zip(NEAR, ("l", "r", "last")):
                send(z, way, ("s5", q), s_y, s_in.at[0])
            give(s_y)
        elif n == 7:
            arrived(("s5", z), s_in.at[0])
            give(s_in.at[0])

    def finish():
        for z in range(NZ):

            @pl.when(zi == z)
            def _(z=z):
                for way, side, core in around:
                    arrived(("s6", way), o_small.at[quarter(side, core)])
                    arrived(("s7", way), o_shared.at[quarter_sh(side, core)])
                for u, (i, first, _, _, roots) in enumerate(UNITS):
                    for k in range(NZ):
                        half = y if first else 0
                        arrived(("cf", u, k, 0), result(u, k, half, 1 - c, x))
                        if first:
                            arrived(("cf", u, k, 1), result(u, k, 1 - y, 1 - c, x))
                        if i == 5:
                            for h in range(2 if first else 1):
                                at = (y if h == 0 else 1 - y) if first else 0
                                arrived(("cf", u, k, 2 + h), result(u, k, at, 1 - c, other))
                        if roots[k] == z:
                            own_copy(u, k, chunk(u, k, half), half).wait()
                for n, shape, dtype in sent[z]:
                    like = g_v.at[0, 0 : shape[0]] if dtype == BF else o_shared.at[0 : shape[0]]
                    pltpu.make_async_remote_copy(
                        src_ref=like, dst_ref=like, send_sem=asend.at[n], recv_sem=arecv.at[n],
                        device_id=(w, other), device_id_type=MESH,
                    ).wait_send()


    c_gout.wait()
    c_up.wait()
    P2 = g_v.shape[2]

    @pl.loop(0, 4)
    def _(i):
        mt = cols(i, 256)
        mf = pl.ds(pl.multiple_of(c * halfF + i * 256, 256), 256)
        la = up[:, mf]
        lb = p_up[:, mt]
        for j in range(2):
            nn = slice(j * P2, (j + 1) * P2)
            g_v[j, mt, :] = (mm_tn(la, gout[:, nn]) + mm_tn(lb, p_gout[:, nn])).astype(BF)

    slot(1)

    @pl.loop(0, D // T)
    def _(i):
        cc = cols(i, T)
        part_s[:, cc] = mm_nt(gpu[oth, :], wup[cc, :]).astype(BF)

    x_gn2 = xcopy(4, part_s, gn2_r)
    x_gn2.start()
    slot(2)

    @pl.loop(0, D // T)
    def _(i):
        cc = cols(i, T)
        own_f[:, cc] = mm_nt(gpu[own, :], wup[cc, :])
        ffn_s[:, cc] = mm(up[oth, :], wdn[:, cc]).astype(BF)
        ffn_o[:, cc] = mm(up[own, :], wdn[:, cc])


    pl.semaphore_signal(ready.at[0], inc=1, device_id=(wy, x), device_id_type=MESH)

    @pl.when(zi > 0)
    def _():
        pl.semaphore_signal(ready.at[2], inc=1, device_id=(wl, x), device_id_type=MESH)

    @pl.when(zi < NZ - 1)
    def _():
        pl.semaphore_signal(ready.at[1], inc=1, device_id=(wr_, x), device_id_type=MESH)

    pl.semaphore_wait(ready.at[0], 1)

    @pl.when(zi > 0)
    def _():
        pl.semaphore_wait(ready.at[1], 1)

    @pl.when(zi < NZ - 1)
    def _():
        pl.semaphore_wait(ready.at[2], 1)

    slot(3)
    c_n2.wait()
    c_gpu.wait()

    @pl.loop(0, 4)
    def _(i):
        mt = cols(i, 256)
        la = n2[:, mt]
        lb = p_n2[:, mt]
        for j in range(2):
            nf = pl.ds(pl.multiple_of(c * halfF + j * P2, P2), P2)
            nn = slice(j * P2, (j + 1) * P2)
            g_v[2 + j, mt, :] = (mm_tn(la, gpu[:, nf]) + mm_tn(lb, p_gpu[:, nn])).astype(BF)

    slot(4)
    x_gn2.wait()

    acc[...] = jnp.zeros_like(acc)

    def add_rows(k, v):
        acc[k * 8 : k * 8 + 8, :] += v[0:8, :] + v[8:16, :]

    def norm2_back(t):
        rr = cols(t, 16)
        ro = pl.ds(pl.multiple_of(x * H + t * 16, 16), 16)
        g = own_f[rr, :] + gn2_r[rr, :].astype(F32)
        cen, rstd = norm_rows(blend[rr, :])
        xh = cen * rstd
        add_rows(0, g * xh)
        add_rows(1, g)
        gy = g * vec[4:5, :]
        gb = rstd * (gy - jnp.mean(gy, axis=-1, keepdims=True) - xh * jnp.mean(gy * xh, axis=-1, keepdims=True))
        gb = gb + gout[ro, :].astype(F32)
        u = gate[rr, :]
        ph = pre_hid[rr, :]
        sg = sigm(ph)
        tk = tok[ro, :].astype(F32)
        gud = (gb * (ph * sg - tk) * u * (1.0 - u)).astype(BF)
        ghd = (gb * u * slope_of(ph, sg)).astype(BF)
        hid[ro, :] = ghd
        upd[ro, :] = gud
        add_rows(2, gud.astype(F32))
        gres[rr, :] = gb * (1.0 - u)

    halves = [pl.ds(pl.multiple_of(x * H + h * (H // 2), H // 2), H // 2) for h in range(2)]
    x_hid = [xcopy((5, 22)[h], hid.at[halves[h]], hid.at[halves[h]]) for h in range(2)]
    pl.loop(0, HT // 2)(norm2_back)
    x_hid[0].start()
    slot(5)
    pl.loop(HT // 2, HT)(norm2_back)
    x_hid[1].start()
    x_upd = xcopy(6, upd.at[own], upd.at[own])
    x_ffn = xcopy(7, ffn_s, ffn_r)

    def put_small(row, k):
        v = jnp.sum(acc[k * 8 : k * 8 + 8, :], axis=0, keepdims=True)
        for j in range(8):
            small[row + j : row + j + 1, :] = v[:, j * 128 : (j + 1) * 128]

    put_small(256 + 32, 0)
    put_small(256 + 40, 1)
    put_small(256 + 24, 2)
    slot(6)

    snap_s[...] = jnp.zeros_like(snap_s)
    snap_r[...] = jnp.zeros_like(snap_r)

    def sense(p, state):
        s, r = state
        k = keep[pl.ds(p, 1), :]
        a = coef(a_s)
        sk = s * k
        return a * sk + xs[cols(p, 8), :] * live[pl.ds(p, 1), :], a * (r * k) + sk

    @pl.when(x == 1)
    def _():
        s_mid, r_mid = lax.fori_loop(0, H, sense, (zeros, zeros), unroll=2)
        snap_s[...] = s_mid.reshape(N * 8, 128)
        snap_r[...] = r_mid.reshape(N * 8, 128)

    for copy in x_hid:
        copy.wait()
    x_upd.start()
    c_hid = ccopy(7, hid, p_hid)
    c_hid.start()
    gp_acc[...] = jnp.zeros_like(gp_acc)

    def gated_back(i):
        cc = cols(i, T)
        gg = mm_nt(hid[...], wm[cc, :])
        pr = pre_r[:, cc]
        sg = sigm(pr)
        ga = (gg * (pr * sg)).astype(BF)
        gpr[:, cc] = (gg * att[:, cc] * slope_of(pr, sg)).astype(BF)
        pv = pre_v[:, cc]
        sv = slope_of(pv, sigm(pv))
        for b in range(2):
            rb = slice(b * BL, (b + 1) * BL)
            gp_acc[rb, :] += mm_nt(ga[rb, :], vlow[rb, cc])
            gv = mm_tn(plow[rb, :], ga[rb, :])
            gpv[rb, cc] = (gv * sv[rb, :]).astype(BF)

    for i in range(VL // T):
        pl.loop(i, i + 1)(gated_back)
        slot(7 + i)
    x_gp = xcopy(8, gp_acc.at[oth], gp_r)
    x_gp.start()
    x_upd.wait()

    @pl.loop(0, D // T)
    def _(i):
        cc = cols(i, T)
        part_s[:, cc] = mm_nt(gpr[oth, :], wr[cc, :]).astype(BF)

    x_mb = xcopy(9, part_s, mb_r)
    x_mb.start()
    slot(11)

    @pl.loop(0, D // T)
    def _(i):
        cc = cols(i, T)
        nb_s[:, cc] = mm_nt(gpv[oth, :], wv[cc, :]).astype(BF)

    x_nb = xcopy(10, nb_s, nb_r)
    halfV = VL // 2
    c_gpr = ccopy(8, gpr.at[:, pl.ds(pl.multiple_of((1 - c) * halfV, halfV), halfV)], p_gpr)
    c_gpv = ccopy(9, gpv.at[:, pl.ds(pl.multiple_of((1 - c) * halfV, halfV), halfV)], p_gpv)
    c_upd = ccopy(10, upd, p_upd)
    c_gpr.start()
    c_gpv.start()
    c_upd.start()

    slot(12)
    c_hid.wait()
    c_gated.wait()
    hv = pl.ds(pl.multiple_of(c * P2, P2), P2)
    q4 = pl.ds(pl.multiple_of((2 * x + c) * 256, 256), 256)

    @pl.loop(0, 4)
    def _(i):
        mt = cols(i, 256)
        g_v[4, mt, :] = (mm_tn(gated[:, mt], hid[:, hv]) + mm_tn(p_gated[:, mt], p_hid[:, hv])).astype(BF)

    slot(13)

    x_gp.wait()
    gpb = gp_acc[own, :] + gp_r[...]
    po = probs[own, :]
    gsc = (po * (gpb - jnp.sum(gpb * po, axis=-1, keepdims=True))).astype(BF)
    gq = mm(gsc, klow[own, :]) * scale
    gk = mm_tn(gsc, qlow[own, :]) * scale
    psh = pre_sh[own, :]
    sgs = sigm(psh)
    sh = psh * sgs
    small[336:337, :] = jnp.sum(gq * sh, axis=0, keepdims=True)
    small[337:338, :] = jnp.sum(gk * sh, axis=0, keepdims=True)
    small[338:339, :] = jnp.sum(gq, axis=0, keepdims=True)
    small[339:340, :] = jnp.sum(gk, axis=0, keepdims=True)
    small[340:341, :] = jnp.sum(skew(gsc.astype(F32).T, True), axis=0, keepdims=True)
    small[341:352, :] = jnp.zeros((11, 128), F32)
    gps[own, :] = ((gq * qkg[0:1, :] + gk * qkg[1:2, :]) * slope_of(psh, sgs)).astype(BF)
    x_gps = xcopy(11, gps.at[own], gps.at[own])
    x_gps.start()
    x_nb.start()
    slot(14)
    c_mixed.wait()
    c_upd.wait()

    la = mlow[:, q4]
    lb = p_mixed[:, q4]
    for j in range(2):
        nn = slice(j * P2, (j + 1) * P2)
        g_v[5, j * 256 : j * 256 + 256, :] = (mm_tn(la, hid[:, nn]) + mm_tn(lb, p_hid[:, nn])).astype(BF)
        g_v[5, 512 + j * 256 : 768 + j * 256, :] = (mm_tn(la, upd[:, nn]) + mm_tn(lb, p_upd[:, nn])).astype(BF)

    slot(15)

    @pl.loop(0, D // T)
    def _(i):
        cc = cols(i, T)
        own_f[:, cc] = (
            mm_nt(gpr[own, :], wr[cc, :])
            + mm_nt(gps[own, :], wsh[cc, :])
            + mm_nt(hid[own, :], wh[cc, :])
            + mm_nt(upd[own, :], wu[cc, :])
        )
        nb_o[:, cc] = mm_nt(gpv[own, :], wv[cc, :])

    slot(16)
    x_gps.wait()
    c_gps = ccopy(11, gps, p_gps)
    c_gps.start()
    c_gpr.wait()

    @pl.loop(0, 4)
    def _(i):
        mt = cols(i, 256)
        g_v[6, mt, :] = (mm_tn(mlow[:, mt], gpr[:, hv]) + mm_tn(p_mixed[:, mt], p_gpr[...])).astype(BF)

    slot(17)
    c_normed.wait()
    c_gpv.wait()

    @pl.loop(0, 4)
    def _(i):
        mt = cols(i, 256)
        g_v[7, mt, :] = (mm_tn(nlow[:, mt], gpv[:, hv]) + mm_tn(p_normed[:, mt], p_gpv[...])).astype(BF)

    c_gps.wait()
    s_own[88:344, :] = mm_tn(mlow[:, q4], gps[...]) + mm_tn(p_mixed[:, q4], p_gps[...])
    slot(18)
    x_mb.wait()
    x_ffn.start()

    acc[...] = jnp.zeros_like(acc)

    @pl.loop(0, H // 16)
    def _(t):
        rr = cols(t, 16)
        ro = pl.ds(pl.multiple_of(x * H + t * 16, 16), 16)
        pre = pre_ema[ro, :]
        g = (own_f[rr, :] + mb_r[rr, :].astype(F32)) * slope_of(pre, sigm(pre))
        own_f[rr, :] = g
        add_rows(0, g * normed[ro, :])
        for j in range(8):
            gs[pl.ds(t * 128 + j, 16, stride=8), :] = g[:, j * 128 : (j + 1) * 128]

    put_small(256, 0)
    slot(19)

    def back(p_, cy):
        p = H - 1 - p_
        at = cols(p, 8)
        po_ = x * H + p
        mu = gs[at, :] + cy
        gxs[at, :] = jnp.sum(coef(w_s) * mu, axis=0) * live[pl.ds(po_, 1), :]
        return coef(a_s) * (mu * keep[pl.ds(po_, 1), :])

    x_carry = xcopy(12, carry, carry_r)

    @pl.when(x == 1)
    def _():
        cy = lax.fori_loop(0, H, back, zeros)
        carry[...] = cy.reshape(N * 8, 128)
        x_carry.start()

    slot(20)
    for q in range(2):
        nq = slice(q * 64, q * 64 + 64)

        def fwd(p, state, nq=nq):
            s, r, gw, gr = state
            at = cols(p, 8)
            po_ = x * H + p
            k = keep[pl.ds(po_, 1), :]
            xr = xs[cols(po_, 8), :] * live[pl.ds(po_, 1), :]
            a = a_s[nq, :].reshape(8, 8, 128)
            sk = s * k
            r = a * (r * k) + sk
            s = a * sk + xr
            g = gs[at, :]
            return s, r, gw + g * s, gr + g * r

        z8 = jnp.zeros((8, 8, 128), F32)
        s0 = snap_s[nq, :].reshape(8, 8, 128)
        r0 = snap_r[nq, :].reshape(8, 8, 128)
        _, _, gw, gr = lax.fori_loop(0, H, fwd, (s0, r0, z8, z8))
        small[nq, :] = gw.reshape(64, 128)
        small[128 + q * 64 : 192 + q * 64, :] = gr.reshape(64, 128) * w_s[nq, :]
        slot(21 + q)

    @pl.when(x == 0)
    def _():
        x_carry.wait_recv()
        lax.fori_loop(0, H, back, coef(carry_r))

    @pl.when(x == 1)
    def _():
        x_carry.wait_send()

    slot(23)
    x_nb.wait()

    @pl.loop(0, H // 16)
    def _(t):
        rr = cols(t, 16)
        ro = pl.ds(pl.multiple_of(x * H + t * 16, 16), 16)
        gx = jnp.concatenate([gxs[pl.ds(t * 128 + j, 16, stride=8), :] for j in range(8)], axis=1)
        g = nb_o[rr, :] + nb_r[rr, :].astype(F32) + vec[2:3, :] * own_f[rr, :] + gx
        cen, rstd = norm_rows(tok[ro, :].astype(F32))
        xh = cen * rstd
        add_rows(1, g * xh)
        add_rows(2, g)
        gy = g * vec[0:1, :]
        gb = rstd * (gy - jnp.mean(gy, axis=-1, keepdims=True) - xh * jnp.mean(gy * xh, axis=-1, keepdims=True))
        gt[rr, :] = gres[rr, :] + gb

    put_small(256 + 8, 1)
    put_small(256 + 16, 2)

    slot(24)

    x_ffn.wait()

    @pl.loop(0, H // 16)
    def _(t):
        rr = cols(t, 16)
        bo[rr, :] = (blend[rr, :] + (ffn_o[rr, :] + ffn_r[rr, :].astype(F32))).astype(BF)

    slot(25)
    finish()

def vm(shape, dtype=F32):
    return pltpu.VMEM(shape, dtype)


SEMS = 440


def run_main(tokens, cotangent, seq_lengths, bucket_map, norm1_gain, norm1_bias, ema_rate, ema_damp, ema_in, ema_out,
             ema_skip, w_shared, qk_gain, qk_bias, rel_bias, w_value, w_reset, w_mix, w_hidden, w_update, b_update,
             norm2_gain, norm2_bias, w_up, b_up, w_down):
    H = tokens.shape[0]
    R = 2 * H
    D = tokens.shape[1]
    VL = w_value.shape[1]
    FL = w_up.shape[1]
    Z = w_shared.shape[1]
    rows8 = [v.reshape(8, D // 8) for v in (norm1_gain, norm1_bias, ema_skip, b_update, norm2_gain, norm2_bias)]
    anyspec = pl.BlockSpec(memory_space=pl.ANY)
    vspec = pl.BlockSpec(memory_space=pltpu.VMEM)
    sspec = pl.BlockSpec(memory_space=pltpu.SMEM)
    P2 = D // 2
    outs = (
        jax.ShapeDtypeStruct((H, D), BF),
        jax.ShapeDtypeStruct((H, D), F32),
        jax.ShapeDtypeStruct((FL, D), BF),
        jax.ShapeDtypeStruct((D, FL), BF),
        jax.ShapeDtypeStruct((VL, D), BF),
        jax.ShapeDtypeStruct((4, D, P2), BF),
        jax.ShapeDtypeStruct((D, VL), BF),
        jax.ShapeDtypeStruct((D, VL), BF),
        jax.ShapeDtypeStruct((D, Z), F32),
        jax.ShapeDtypeStruct((352, 128), F32),
    )
    dma = pltpu.SemaphoreType.DMA
    scratch = [
        vm((D, Z), BF), vm((D, VL), BF), vm((D, VL), BF), vm((VL, D), BF), vm((D, D), BF), vm((D, D), BF), vm((D, FL), BF), vm((FL, D), BF),
        vm((R, D), BF), vm((R, D), BF), vm((R, D)), vm((R, D), BF), vm((R, D), BF), vm((R, D)), vm((R * 8, 128)), vm((R * 8, 128)),
        vm((R, Z)), vm((R, Z), BF), vm((R, Z), BF), vm((R, BLOCK)), vm((R, BLOCK), BF),
        vm((R, VL)), vm((R, VL)), vm((R, VL)), vm((R, VL), BF), vm((R, VL), BF), vm((H, D), BF), vm((H, D), BF), vm((H, D)), vm((H, D)), vm((H, D)), vm((H, D)), vm((R, D), BF),
        vm((R, FL)), vm((R, FL), BF), vm((R, FL), BF), vm((H, D), BF), vm((H, D), BF), vm((H, D), BF), vm((R, D), BF), vm((R, D), BF), vm((R, VL), BF), vm((R, VL), BF), vm((R, BLOCK)), vm((H, BLOCK)), vm((R, Z), BF),
        vm((H, D), BF), vm((H, D), BF), vm((H, D), BF),
        vm((R, D), BF), vm((R, D), BF), vm((R, D), BF), vm((R, FL // 2), BF), vm((R, D), BF), vm((R, FL // 2), BF), vm((R, VL), BF), vm((R, D), BF), vm((R, D), BF), vm((R, VL // 2), BF), vm((R, VL // 2), BF), vm((R, Z), BF),
        vm((128, 128)), vm((128, 128)), vm((128, 128)), vm((128, 128)), vm((128, 128)), vm((128, 128)), vm((24, D)), vm((R, 128)), vm((R, 128)), vm((R, 128)), vm((8, D)), vm((8, FL)),
        vm((8, D, P2), BF), vm((11 * 256, P2), BF), vm((352, 128)), vm((3, 88, 128)), vm((344, 128)), vm((344, 128)), vm((NZ - 1, 344, 128)),
        dma((10,)), dma((23,)), dma((23,)), dma((12,)), dma((12,)), dma((96,)), dma((SEMS,)), dma((SEMS,)), pltpu.SemaphoreType.REGULAR((3,)),
    ]
    return pl.pallas_call(
        main_kernel,
        out_shape=outs,
        in_specs=[anyspec] * 10 + [sspec, sspec] + [vspec] * 14,
        out_specs=(vspec, vspec) + (anyspec,) * 6 + (vspec, vspec),
        scratch_shapes=scratch,
        compiler_params=pltpu.CompilerParams(collective_id=0, has_side_effects=True, vmem_limit_bytes=63 * 1024 * 1024),
        cost_estimate=pl.CostEstimate(flops=15_000_000_000, bytes_accessed=40_000_000, transcendentals=0),
    )(
        tokens, cotangent, w_shared, w_value, w_reset, w_mix, w_hidden, w_update, w_up, w_down,
        seq_lengths, rel_bias.reshape(1, -1), bucket_map.reshape(1, -1), *rows8, ema_rate, ema_damp, ema_in, ema_out,
        qk_gain, qk_bias, b_up.reshape(-1, 128),
    )


def finish_kernel(down, up, mix, reset, value, h0, h1, u0, u1, small, rate, damp, ein, eout, bmap, bo, gt, shared,
                  f_down, f_up, f_mix, f_reset, f_value, f_hid, f_upd, g_rate, g_damp, g_in, g_out, v0, v1, v2, v3, v4, v5, g_bup, g_gain, g_bias, g_rel, f_bo, f_gt, f_shared):
    for src, dst in ((down, f_down), (up, f_up), (mix, f_mix), (reset, f_reset), (value, f_value)):
        dst[...] = src[...].astype(F32)
    half = h0.shape[2]
    for left, right, dst in ((h0, h1, f_hid), (u0, u1, f_upd)):
        dst[:, 0:half] = left[0].astype(F32)
        dst[:, half : 2 * half] = right[0].astype(F32)

    @pl.when(pl.program_id(0) == 0)
    def _():
        for t in range(2):
            for j in range(8):
                rows_ = slice(t * 8, t * 8 + 8)
                lanes = slice(j * 128, j * 128 + 128)
                gw = small[pl.ds(t * 64 + j, 8, stride=8), :]
                ga = small[pl.ds(128 + t * 64 + j, 8, stride=8), :]
                r_, d_ = rate[rows_, lanes], damp[rows_, lanes]
                i_, o_ = ein[rows_, lanes], eout[rows_, lanes]
                g_rate[rows_, lanes] = gw * (i_ * o_) - ga * d_
                g_damp[rows_, lanes] = -ga * r_
                g_in[rows_, lanes] = gw * (r_ * o_)
                g_out[rows_, lanes] = gw * (r_ * i_)
        for k, ref in enumerate((v0, v1, v2, v3, v4, v5)):
            ref[...] = small[256 + 8 * k : 264 + 8 * k, :]
        f_bo[...] = bo[...]
        f_gt[...] = gt[...]
        f_shared[...] = shared[...]
        me = lax.axis_index("narrow")
        g_bup[...] = small[pl.ds(pl.multiple_of(304 + me * 16, 8), 16), :]
        g_gain[...] = small[336:338, :]
        g_bias[...] = small[338:340, :]
        n = bmap.shape[1]
        offs = jnp.broadcast_to(small[340:341, :], (n, n)).T
        which = jnp.broadcast_to(bmap[...].astype(F32), (n, n)).T
        lane = lax.broadcasted_iota(jnp.int32, (n, n), 1).astype(F32)
        hits = jnp.sum(jnp.where(which == lane, offs, 0.0), axis=0, keepdims=True)
        g_rel[...] = hits[:, 0 : g_rel.shape[1]]


def run_finish(grads, hu, whole, small, rate, damp, ein, eout, bucket_map, nbuck):
    steps = 8

    def part(a):
        return pl.BlockSpec((a.shape[0] // steps, a.shape[1]), lambda i: (i, 0))

    def full(shape):
        return pl.BlockSpec(shape, lambda i: (0,) * len(shape))

    bmap = bucket_map.reshape(1, -1)
    D = rate.shape[1]
    square = jax.ShapeDtypeStruct((D, D), F32)
    outs = [jax.ShapeDtypeStruct(a.shape, F32) for a in grads] + [square, square]
    per = steps // 4
    hu_specs = [pl.BlockSpec((1, D // steps, D // 2), lambda i, b=b: (i // per, b * per + i % per, 0)) for b in range(4)]
    outs += [jax.ShapeDtypeStruct(rate.shape, F32) for _ in range(4)]
    outs += [jax.ShapeDtypeStruct((8, 128), F32) for _ in range(6)]
    outs += [jax.ShapeDtypeStruct((16, 128), F32), jax.ShapeDtypeStruct((2, 128), F32), jax.ShapeDtypeStruct((2, 128), F32),
             jax.ShapeDtypeStruct((1, nbuck), F32)]
    outs += [jax.ShapeDtypeStruct(a.shape, a.dtype) for a in whole]
    smalls = (small, rate, damp, ein, eout, bmap) + tuple(whole)
    return pl.pallas_call(
        finish_kernel,
        grid=(steps,),
        out_shape=tuple(outs),
        in_specs=[part(a) for a in grads] + hu_specs + [full(a.shape) for a in smalls],
        out_specs=tuple([part(a) for a in outs[:7]] + [full(o.shape) for o in outs[7:]]),
        compiler_params=pltpu.CompilerParams(vmem_limit_bytes=60 * 1024 * 1024),
    )(*grads, hu, hu, hu, hu, *smalls)


def shards_fast(*args):
    bo, gt, down, up, mix, hu, reset, value, shared, small = run_main(*args)
    (tokens, cotangent, seq_lengths, bucket_map, norm1_gain, norm1_bias, ema_rate, ema_damp, ema_in, ema_out,
     ema_skip, w_shared, qk_gain, qk_bias, rel_bias) = args[:15]
    (down, up, mix, reset, value, hidden, update, g_rate, g_damp, g_in, g_out, skip, n1g, n1b, bupd, n2g, n2b,
     g_bup, g_gain, g_bias, g_rel, bo, gt, shared) = run_finish(
        (down, up, mix, reset, value), hu, (bo, gt, shared), small, ema_rate, ema_damp, ema_in, ema_out, bucket_map,
        rel_bias.shape[0])
    skip, n1g, n1b, bupd, n2g, n2b = [v.reshape(-1) for v in (skip, n1g, n1b, bupd, n2g, n2b)]
    return (bo, gt, n1g, n1b, g_rate, g_damp, g_in, g_out, skip, shared, g_gain, g_bias, g_rel.reshape(-1),
            value, reset, mix, hidden, update, bupd, n2g, n2b, up, g_bup.reshape(-1), down)


def solution(mesh):
    in_specs = (
        P(("wide", "narrow"), None),
        P(("wide", "narrow"), None),
        P("wide", None),
        P(),
        P(),
        P(),
        P(),
        P(),
        P(),
        P(),
        P(),
        P(),
        P(),
        P(),
        P(),
        P(None, "narrow"),
        P(None, "narrow"),
        P("narrow", None),
        P(),
        P(),
        P(),
        P(),
        P(),
        P(None, "narrow"),
        P("narrow"),
        P("narrow", None),
    )
    out_specs = (
        P(("wide", "narrow"), None),
        P(("wide", "narrow"), None),
        P(),
        P(),
        P(),
        P(),
        P(),
        P(),
        P(),
        P(),
        P(),
        P(),
        P(),
        P(None, "narrow"),
        P(None, "narrow"),
        P("narrow", None),
        P(),
        P(),
        P(),
        P(),
        P(),
        P(None, "narrow"),
        P("narrow"),
        P("narrow", None),
    )
    body = shards_fast if (mesh.shape["wide"], mesh.shape["narrow"]) == (16, 2) else shards
    return jax.shard_map(body, mesh=mesh, in_specs=in_specs, out_specs=out_specs, check_vma=False)
```

profile of v0, /device:TPU:1, one launch (start us, length us, event | category | flops | bytes accessed | tf_op | source)
XLA Modules:
  0.0 223.1 jit_solution(1873562407649343755)
XLA Ops:
  0.7 200.7 %shard_map.433 = (bf16[128,1024]{1,0:T(8,128)(2,1)}, f32[128,1024]{1,0:T(8,128)}, bf16[2048,1024]{1,0:T(8,128)(2,1)}, bf16[1024,2048]{1,0:T(8,128)(2,1)}, bf16[1...) custom-call(bf16[128,1024]{1,0:T(8,128)(2,1)} %tok_h.1, ...), custom_call_target="tpu_custom_call" | custom-call | flops 15000000512 | bytes 40000000 | tf_op jit(solution)/shard_map/pallas_call | solution.py:1581
  201.4 21.5 %shard_map.434 = (f32[2048,1024]{1,0:T(8,128)}, f32[1024,2048]{1,0:T(8,128)}, f32[1024,1024]{1,0:T(8,128)}, f32[1024,1024]{1,0:T(8,128)}, f32[1024,1024]{1,0:T(8...) custom-call(bf16[2048,1024]{1,0:T(8,128)(2,1)} %get-tuple-element.58, ...), custom_call_target="tpu_custom_call" | custom-call | tf_op jit(solution)/shard_map/pallas_call | solution.py:1657
where the time goes:
time: 223 us
  Pallas kernels  222 us (100%)
    pallas_call x1, Pallas kernels, run_main(): pl.pallas_call(main_kernel, out_shape=outs, in_specs=[anyspec] * 10 + [ss...  201 us
    pallas_call x1, Pallas kernels, run_finish(): pl.pallas_call(finish_kernel, grid=(steps,), out_shape=tuple(outs), in_sp...  21.5 us

commit v1 on v0

--- a/solution.py
+++ b/solution.py
@@ -403,16 +403,16 @@
 EVEN, ENDS = (0, 1, 2, 3), (0, 3, 0, 3)
 MIXED = (0, 3, 1, 2)
 UNITS = (
-    (0, 1, 0, 512, ENDS), (0, 0, 512, 512, MIXED), (1, 2, 0, 512, EVEN), (1, 0, 512, 512, ENDS), (2, 0, 0, 256, ENDS), (2, 1, 256, 768, ENDS),
-    (3, 1, 0, 768, EVEN), (3, 1, 768, 256, MIXED), (4, 1, 0, 768, ENDS), (4, 1, 768, 256, ENDS), (5, 2, 0, 512, EVEN), (5, 0, 512, 512, EVEN),
-    (6, 2, 0, 256, ENDS), (6, 2, 256, 768, ENDS), (7, 1, 0, 512, ENDS), (7, 1, 512, 512, ENDS),
+    (0, 1, 0, 512, ENDS), (0, 0, 512, 512, MIXED), (1, 0, 0, 512, ENDS), (1, 2, 512, 512, EVEN), (2, 1, 0, 1024, EVEN), (3, 1, 0, 1024, ENDS),
+    (4, 1, 0, 1024, MIXED), (5, 0, 0, 512, MIXED), (5, 0, 512, 512, MIXED), (6, 1, 0, 256, EVEN), (6, 2, 256, 768, ENDS),
+    (7, 1, 0, 512, ENDS), (7, 1, 512, 512, ENDS),
 )
-PHASES = (1.5, 1.0, 2.0, 1.5, 3.5, 1.2, 5.5, 1.5, 1.5, 1.5, 1.0, 1.0, 0.8, 1.5, 0.8, 2.0, 0.8, 1.0, 2.0, 1.3, 1.3, 1.3, 1.3, 4.0, 1.0)
+PHASES = (1.8, 1.2, 2.4, 1.8, 4.2, 1.4, 6.6, 1.8, 1.8, 1.8, 1.2, 1.2, 1.0, 1.8, 1.0, 2.4, 1.0, 1.2, 2.4, 1.6, 1.6, 1.6, 1.6, 4.8, 1.2)
 RELEASE = {0: 0, 1: 0, 2: 3, 3: 3, 4: 12, 5: 14, 6: 16, 7: 17}
 EARLY = tuple(u for u, t in enumerate(UNITS) if t[0] < 2)
 UNIT, LAG = 3.0, 2.0
 MARGIN, WINDOW = 0.0, 1000.0
-RANKS = {"G": 1, "P": 1, "C": 1, "D": 1, "F": 1, "W": 1, "Y": 4, "X": 4, "S": 0}
+RANKS = {"G": 1, "P": 1, "C": 1, "D": 1, "F": 2, "W": 2, "Y": 4, "X": 4, "S": 0}
 BY_UNIT = False
 
 
@@ -522,7 +522,7 @@
             key, _, _, _, out, cost = item
             done[z].add(key)
             plan[z][phase[z]].append(key)
-            clock[z] += cost
+            clock[z] += 0.8 * cost
             for lane, dest, message, size in out:
                 begin = max(link.get((z, lane), 0.0), clock[z])
                 took = size * UNIT * (0.2 if lane == "c" else 1.0)
@@ -697,7 +697,7 @@
 
     HT = H // 16
     wcopies[0].wait()
-    pl.loop(0, HT)(lambda t: norm1(x * HT + t))
+    pl.loop(0, HT, unroll=2)(lambda t: norm1(x * HT + t))
     N = 16
 
     def coef(ref):
@@ -737,10 +737,10 @@
         @pl.when(x == (1 if j < 4 else 0))
         def _(j=j):
             x_tok[j % 4].wait_recv()
-            pl.loop(j * (HC // 16), (j + 1) * (HC // 16))(norm1)
+            pl.loop(j * (HC // 16), (j + 1) * (HC // 16), unroll=2)(norm1)
 
         state = lax.fori_loop(j * HC, (j + 1) * HC, forward, state, unroll=4)
-        pl.loop(j * (HC // 16), (j + 1) * (HC // 16))(mixed_rows)
+        pl.loop(j * (HC // 16), (j + 1) * (HC // 16), unroll=2)(mixed_rows)
 
     for copy in x_tok:
         copy.wait_send()
@@ -844,8 +844,8 @@
 
 
     def blend_rows(t):
-        rr = cols(t, 16)
-        ro = pl.ds(pl.multiple_of(x * H + t * 16, 16), 16)
+        rr = cols(t, 32)
+        ro = pl.ds(pl.multiple_of(x * H + t * 32, 32), 32)
         ph = pre_hid[rr, :] + (own_f[rr, :] + mix_r[rr, :].astype(F32))
         pre_hid[rr, :] = ph
         u = gate[rr, :]
@@ -858,7 +858,7 @@
     for h in range(4):
         if h % 2 == 0:
             x_mix[h // 2].wait()
-        pl.loop(h * (HT // 4), (h + 1) * (HT // 4))(blend_rows)
+        pl.loop(h * (H // 128), (h + 1) * (H // 128))(blend_rows)
         part = pl.ds(pl.multiple_of(x * H + h * (H // 4), H // 4), H // 4)
         x_n2.append(xcopy(3 if h == 0 else 13 + h, n2.at[part], n2.at[part]))
         x_n2[h].start()
@@ -1593,83 +1593,118 @@
     )
 
 
-def finish_kernel(down, up, mix, reset, value, h0, h1, u0, u1, small, rate, damp, ein, eout, bmap, bo, gt, shared,
-                  f_down, f_up, f_mix, f_reset, f_value, f_hid, f_upd, g_rate, g_damp, g_in, g_out, v0, v1, v2, v3, v4, v5, g_bup, g_gain, g_bias, g_rel, f_bo, f_gt, f_shared):
-    for src, dst in ((down, f_down), (up, f_up), (mix, f_mix), (reset, f_reset), (value, f_value)):
-        dst[...] = src[...].astype(F32)
-    half = h0.shape[2]
-    for left, right, dst in ((h0, h1, f_hid), (u0, u1, f_upd)):
-        dst[:, 0:half] = left[0].astype(F32)
-        dst[:, half : 2 * half] = right[0].astype(F32)
-
-    @pl.when(pl.program_id(0) == 0)
-    def _():
-        for t in range(2):
-            for j in range(8):
-                rows_ = slice(t * 8, t * 8 + 8)
-                lanes = slice(j * 128, j * 128 + 128)
-                gw = small[pl.ds(t * 64 + j, 8, stride=8), :]
-                ga = small[pl.ds(128 + t * 64 + j, 8, stride=8), :]
-                r_, d_ = rate[rows_, lanes], damp[rows_, lanes]
-                i_, o_ = ein[rows_, lanes], eout[rows_, lanes]
-                g_rate[rows_, lanes] = gw * (i_ * o_) - ga * d_
-                g_damp[rows_, lanes] = -ga * r_
-                g_in[rows_, lanes] = gw * (r_ * o_)
-                g_out[rows_, lanes] = gw * (r_ * i_)
-        for k, ref in enumerate((v0, v1, v2, v3, v4, v5)):
-            ref[...] = small[256 + 8 * k : 264 + 8 * k, :]
-        f_bo[...] = bo[...]
-        f_gt[...] = gt[...]
-        f_shared[...] = shared[...]
-        me = lax.axis_index("narrow")
-        g_bup[...] = small[pl.ds(pl.multiple_of(304 + me * 16, 8), 16), :]
-        g_gain[...] = small[336:338, :]
-        g_bias[...] = small[338:340, :]
-        n = bmap.shape[1]
-        offs = jnp.broadcast_to(small[340:341, :], (n, n)).T
-        which = jnp.broadcast_to(bmap[...].astype(F32), (n, n)).T
-        lane = lax.broadcasted_iota(jnp.int32, (n, n), 1).astype(F32)
-        hits = jnp.sum(jnp.where(which == lane, offs, 0.0), axis=0, keepdims=True)
-        g_rel[...] = hits[:, 0 : g_rel.shape[1]]
+def finish_kernel(down, up, mix, reset, value, hu, bo, gt, shared, small, rate, damp, ein, eout, bmap,
+                  f_down, f_up, f_mix, f_reset, f_value, f_hid, f_upd, f_bo, f_gt, f_shared,
+                  g_rate, g_damp, g_in, g_out, v0, v1, v2, v3, v4, v5, g_bup, g_gain, g_bias, g_rel,
+                  b_down, b_up, b_mix, b_reset, b_value, b_hu, b_bo, b_gt, b_shared, stage, isem, osem, psem):
+    rows_in = [pltpu.make_async_copy(a, b, psem.at[k]) for k, (a, b) in enumerate(((bo, b_bo), (gt, b_gt), (shared, b_shared)))]
+    passed = [pltpu.make_async_copy(a, b, psem.at[3 + k]) for k, (a, b) in enumerate(((b_bo, f_bo), (b_gt, f_gt), (b_shared, f_shared)))]
+    CR, CC = stage.shape[1], stage.shape[2]
+    chunks = []
+    for src, buf, dst in ((down, b_down, f_down), (up, b_up, f_up), (mix, b_mix, f_mix), (reset, b_reset, f_reset), (value, b_value, f_value)):
+        for r in range(src.shape[0] // CR):
+            for q in range(src.shape[1] // CC):
+                at = (slice(r * CR, (r + 1) * CR), slice(q * CC, (q + 1) * CC))
+                chunks.append(([(src.at[at], buf.at[at], slice(0, CC))], dst.at[at]))
+    half = CC // 2
+    for n, dst in ((0, f_hid), (2, f_upd)):
+        for q in range(4):
+            parts = []
+            for j in range(2):
+                at = (q, slice((n + j) * CR, (n + j + 1) * CR))
+                parts.append((hu.at[at], b_hu.at[at], slice(j * half, (j + 1) * half)))
+            chunks.append((parts, dst.at[q * CR : (q + 1) * CR]))
+    ins, count = [], 0
+    for parts, _ in chunks:
+        ins.append([])
+        for src, buf, _ in parts:
+            copy = pltpu.make_async_copy(src, buf, isem.at[count])
+            copy.start()
+            ins[-1].append(copy)
+            count += 1
+    for copy in rows_in:
+        copy.start()
+
+    for t in range(2):
+        for j in range(8):
+            rows_ = slice(t * 8, t * 8 + 8)
+            lanes = slice(j * 128, j * 128 + 128)
+            gw = small[pl.ds(t * 64 + j, 8, stride=8), :]
+            ga = small[pl.ds(128 + t * 64 + j, 8, stride=8), :]
+            r_, d_ = rate[rows_, lanes], damp[rows_, lanes]
+            i_, o_ = ein[rows_, lanes], eout[rows_, lanes]
+            g_rate[rows_, lanes] = gw * (i_ * o_) - ga * d_
+            g_damp[rows_, lanes] = -ga * r_
+            g_in[rows_, lanes] = gw * (r_ * o_)
+            g_out[rows_, lanes] = gw * (r_ * i_)
+    for k, ref in enumerate((v0, v1, v2, v3, v4, v5)):
+        ref[...] = small[256 + 8 * k : 264 + 8 * k, :]
+    me = lax.axis_index("narrow")
+    g_bup[...] = small[pl.ds(pl.multiple_of(304 + me * 16, 8), 16), :]
+    g_gain[...] = small[336:338, :]
+    g_bias[...] = small[338:340, :]
+    n = bmap.shape[1]
+    offs = jnp.broadcast_to(small[340:341, :], (n, n)).T
+    which = jnp.broadcast_to(bmap[...].astype(F32), (n, n)).T
+    lane = lax.broadcasted_iota(jnp.int32, (n, n), 1).astype(F32)
+    hits = jnp.sum(jnp.where(which == lane, offs, 0.0), axis=0, keepdims=True)
+    g_rel[...] = hits[:, 0 : g_rel.shape[1]]
+
+    ring = stage.shape[0]
+    outs = []
+    for k, (parts, dst) in enumerate(chunks):
+        if k >= ring:
+            outs[k - ring].wait()
+        for copy, (_, buf, at) in zip(ins[k], parts):
+            copy.wait()
+
+            @pl.loop(0, CR // 64)
+            def _(t, buf=buf, at=at, k=k):
+                rr = cols(t, 64)
+                stage[k % ring, rr, at] = buf[rr, :].astype(F32)
+
+        copy = pltpu.make_async_copy(stage.at[k % ring], dst, osem.at[k % ring])
+        copy.start()
+        outs.append(copy)
+    for a, b in zip(rows_in, passed):
+        a.wait()
+        b.start()
+    for copy in outs[len(chunks) - ring :] + passed:
+        copy.wait()
 
 
 def run_finish(grads, hu, whole, small, rate, damp, ein, eout, bucket_map, nbuck):
-    steps = 8
-
-    def part(a):
-        return pl.BlockSpec((a.shape[0] // steps, a.shape[1]), lambda i: (i, 0))
-
-    def full(shape):
-        return pl.BlockSpec(shape, lambda i: (0,) * len(shape))
-
     bmap = bucket_map.reshape(1, -1)
     D = rate.shape[1]
     square = jax.ShapeDtypeStruct((D, D), F32)
     outs = [jax.ShapeDtypeStruct(a.shape, F32) for a in grads] + [square, square]
-    per = steps // 4
-    hu_specs = [pl.BlockSpec((1, D // steps, D // 2), lambda i, b=b: (i // per, b * per + i % per, 0)) for b in range(4)]
+    outs += [jax.ShapeDtypeStruct(a.shape, a.dtype) for a in whole]
+    kept = len(outs)
     outs += [jax.ShapeDtypeStruct(rate.shape, F32) for _ in range(4)]
     outs += [jax.ShapeDtypeStruct((8, 128), F32) for _ in range(6)]
     outs += [jax.ShapeDtypeStruct((16, 128), F32), jax.ShapeDtypeStruct((2, 128), F32), jax.ShapeDtypeStruct((2, 128), F32),
              jax.ShapeDtypeStruct((1, nbuck), F32)]
-    outs += [jax.ShapeDtypeStruct(a.shape, a.dtype) for a in whole]
-    smalls = (small, rate, damp, ein, eout, bmap) + tuple(whole)
-    return pl.pallas_call(
+    anyspec = pl.BlockSpec(memory_space=pl.ANY)
+    vspec = pl.BlockSpec(memory_space=pltpu.VMEM)
+    dma = pltpu.SemaphoreType.DMA
+    ring = 14
+    res = pl.pallas_call(
         finish_kernel,
-        grid=(steps,),
         out_shape=tuple(outs),
-        in_specs=[part(a) for a in grads] + hu_specs + [full(a.shape) for a in smalls],
-        out_specs=tuple([part(a) for a in outs[:7]] + [full(o.shape) for o in outs[7:]]),
+        in_specs=[anyspec] * (len(grads) + 4) + [vspec] * 6,
+        out_specs=tuple([anyspec] * kept + [vspec] * (len(outs) - kept)),
+        scratch_shapes=[vm(a.shape, BF) for a in grads] + [vm(hu.shape, BF)] + [vm(a.shape, a.dtype) for a in whole] + [vm((ring, D // 4, D)), dma((44,)), dma((ring,)), dma((6,))],
         compiler_params=pltpu.CompilerParams(vmem_limit_bytes=60 * 1024 * 1024),
-    )(*grads, hu, hu, hu, hu, *smalls)
+    )(*grads, hu, *whole, small, rate, damp, ein, eout, bmap)
+    return res
 
 
 def shards_fast(*args):
     bo, gt, down, up, mix, hu, reset, value, shared, small = run_main(*args)
     (tokens, cotangent, seq_lengths, bucket_map, norm1_gain, norm1_bias, ema_rate, ema_damp, ema_in, ema_out,
      ema_skip, w_shared, qk_gain, qk_bias, rel_bias) = args[:15]
-    (down, up, mix, reset, value, hidden, update, g_rate, g_damp, g_in, g_out, skip, n1g, n1b, bupd, n2g, n2b,
-     g_bup, g_gain, g_bias, g_rel, bo, gt, shared) = run_finish(
+    (down, up, mix, reset, value, hidden, update, bo, gt, shared, g_rate, g_damp, g_in, g_out, skip, n1g, n1b, bupd, n2g, n2b,
+     g_bup, g_gain, g_bias, g_rel) = run_finish(
         (down, up, mix, reset, value), hu, (bo, gt, shared), small, ema_rate, ema_damp, ema_in, ema_out, bucket_map,
         rel_bias.shape[0])
     skip, n1g, n1b, bupd, n2g, n2b = [v.reshape(-1) for v in (skip, n1g, n1b, bupd, n2g, n2b)]

time: 223 us -> 222 us (level)
  no operation moved by 1% of the time
where the time goes in v1:
time: 222 us
  Pallas kernels  221 us (100%)
    pallas_call x1, Pallas kernels, run_main(): pl.pallas_call(main_kernel, out_shape=outs, in_specs=[anyspec] * 10 + [ss...  200 us
    pallas_call x1, Pallas kernels, run_finish(): pl.pallas_call(finish_kernel, out_shape=tuple(outs), in_specs=[anyspec] *...  21.1 us

profile of v1, /device:TPU:1, one launch (start us, length us, event | category | flops | bytes accessed | tf_op | source)
XLA Modules:
  0.0 222.3 jit_solution(6983556266467659469)
XLA Ops:
  0.7 200.3 %shard_map.433 = (bf16[128,1024]{1,0:T(8,128)(2,1)}, f32[128,1024]{1,0:T(8,128)}, bf16[2048,1024]{1,0:T(8,128)(2,1)}, bf16[1024,2048]{1,0:T(8,128)(2,1)}, bf16[1...) custom-call(bf16[128,1024]{1,0:T(8,128)(2,1)} %tok_h.1, ...), custom_call_target="tpu_custom_call" | custom-call | flops 15000000512 | bytes 40000000 | tf_op jit(solution)/shard_map/pallas_call | solution.py:1581
  201.0 21.1 %shard_map.434 = (f32[2048,1024]{1,0:T(8,128)}, f32[1024,2048]{1,0:T(8,128)}, f32[1024,1024]{1,0:T(8,128)}, f32[1024,1024]{1,0:T(8,128)}, f32[1024,1024]{1,0:T(8...) custom-call(bf16[2048,1024]{1,0:T(8,128)(2,1)} %get-tuple-element.58, ...), custom_call_target="tpu_custom_call" | custom-call | tf_op jit(solution)/shard_map/pallas_call | solution.py:1691

commit v2 on v1

--- a/solution.py
+++ b/solution.py
@@ -568,7 +568,7 @@
 def main_kernel(
     tok_h, cot_h, wsh_h, wv_h, wr_h, wm_h, wh_h, wu_h, wup_h, wdn_h,
     lens, relb, bmap, in_n1g, in_n1b, in_skip, in_bupd, in_n2g, in_n2b, rate, damp, ein, eout, qkg, qkb, in_bup,
-    bo, gt, o_down, o_up, o_mix, o_hu, o_reset, o_value, o_shared, o_small,
+    bo, gt, o_all, o_hu, o_shared, o_small,
     wsh, wv, wr, wm, wh, wu, wup, wdn,
     tok, gout, normed, nlow, mlow, pre_ema, xs, smo, pre_sh, qlow, klow, probs, plow,
     pre_v, att, pre_r, vlow, gated, part_s, mix_r, own_f, pre_hid, gate, blend, n2,
@@ -595,14 +595,16 @@
     oth = pl.ds(pl.multiple_of(other * H, H), H)
     D = 1024
     VL = wv.shape[1]
-    FL = wup.shape[1]
+    FL = wup.shape[0] * wup.shape[2]
     EPS = EPSILON
 
     weights = [
-        (tok_h, tok.at[own]), (cot_h, gout.at[own]), (wsh_h, wsh), (wv_h, wv), (wr_h, wr), (wm_h, wm), (wh_h, wh), (wu_h, wu), (wdn_h, wdn),
-        (wup_h, wup),
+        (tok_h, tok.at[own]), (cot_h, gout.at[own]), (wsh_h, wsh), (wv_h, wv), (wr_h, wr), (wm_h, wm), (wh_h, wh), (wu_h, wu),
     ]
     wcopies = [pltpu.make_async_copy(s, d, wsem.at[i]) for i, (s, d) in enumerate(weights)]
+    FB = D // 2
+    down_copies = [pltpu.make_async_copy(wdn_h.at[:, b * FB : (b + 1) * FB], wdn.at[b], wsem.at[8 + b]) for b in range(D // FB)]
+    up_copies = [pltpu.make_async_copy(wup_h.at[:, b * FB : (b + 1) * FB], wup.at[b], wsem.at[10 + b]) for b in range(FL // FB)]
     wcopies[0].start()
     wcopies[1].start()
 
@@ -644,7 +646,7 @@
     x_cot = xcopy(1, cot_h, gout.at[own])
     for copy in x_tok:
         copy.start()
-    for copy in wcopies[2:]:
+    for copy in wcopies[2:] + down_copies + up_copies:
         copy.start()
 
     gs = smo.at[0 : H * 8]
@@ -835,12 +837,13 @@
 
     c_gout = ccopy(3, gout, p_gout)
     c_gout.start()
-    wcopies[8].wait()
+    for copy in down_copies:
+        copy.wait()
 
     @pl.loop(0, FL // T, unroll=2)
     def _(i):
         cc = cols(i, T)
-        gup[:, cc] = mm_nt(gout[...], wdn[cc, :])
+        gup[:, cc] = mm_nt(gout[:, 0:FB], wdn[0, cc, :]) + mm_nt(gout[:, FB:D], wdn[1, cc, :])
 
 
     def blend_rows(t):
@@ -863,12 +866,13 @@
         x_n2.append(xcopy(3 if h == 0 else 13 + h, n2.at[part], n2.at[part]))
         x_n2[h].start()
 
-    wcopies[9].wait()
+    for copy in up_copies:
+        copy.wait()
     FT = FL // T
 
     def up_tile(i, rows_, first):
         cc = cols(i, T)
-        pu = mm(n2[rows_, :], wup[:, cc]) + bup[0:1, cc]
+        pu = mm(n2[rows_, :], wup[i // 2, :, cols(i % 2, T)]) + bup[0:1, cc]
         sg = sigm(pu)
         up[rows_, cc] = (pu * sg).astype(BF)
         gp = (gup[rows_, cc] * slope_of(pu, sg)).astype(BF)
@@ -904,19 +908,18 @@
     def number(*key):
         return numbers.setdefault(key, len(numbers))
 
-    shelves = [[wup, 0, j, 0] for j in range(wup.shape[1] // P2)]
-    shelves += [[wdn, 0, j, 0] for j in range(wdn.shape[1] // P2)] + [[ext, 0, 0, 0]]
+    shelves = [[wup, 0, b] for b in range(wup.shape[0])] + [[wdn, 0, b] for b in range(wdn.shape[0])] + [[ext, 0, 0]]
     places = {}
 
     def place_of(key, n):
         if key not in places:
             for shelf in shelves:
-                if (shelf[0] is ext) == (key[0] in EARLY) and shelf[1] + n <= shelf[0].shape[0]:
-                    places[key] = (shelf[0], shelf[1], shelf[2] * P2)
+                if (shelf[0] is ext) == (key[0] in EARLY) and shelf[1] + n <= shelf[0].shape[1]:
+                    places[key] = (shelf[0], shelf[1], shelf[2])
                     shelf[1] += n
                     break
-        ref, r0, c0 = places[key]
-        return ref.at[r0 : r0 + n, c0 : c0 + P2]
+        ref, r0, b = places[key]
+        return ref.at[b, r0 : r0 + n]
 
     def chunk_rows(u):
         _, first, _, rows, _ = UNITS[u]
@@ -956,18 +959,10 @@
 
     def result(u, k, half, core, side):
         i = UNITS[u][0]
-        n = chunk_rows(u)
-        r0 = first_row(u, k, half)
-        j = i % 2
-        if i < 2:
-            return o_down.at[pl.ds(pl.multiple_of(core * D + r0, 16), n), j * P2 : (j + 1) * P2]
-        rr = pl.ds(pl.multiple_of(r0, 16), n)
-        if i < 4:
-            return o_up.at[rr, pl.ds(pl.multiple_of(core * D + j * P2, P2), P2)]
+        rr = rows_at(u, k, half)
         if i == 5:
             return o_hu.at[2 * side + core, rr]
-        ref = {4: o_mix, 6: o_reset, 7: o_value}[i]
-        return ref.at[rr, pl.ds(pl.multiple_of(core * P2, P2), P2)]
+        return o_all.at[core, i - (i > 5), rr]
 
     sent = [[] for _ in range(NZ)]
 
@@ -1183,10 +1178,14 @@
 
     slot(1)
 
+    def up_back(rows_, cc):
+        parts = [mm_nt(gpu[rows_, b * FB : (b + 1) * FB], wup[b, cc, :]) for b in range(FL // FB)]
+        return (parts[0] + parts[1]) + (parts[2] + parts[3])
+
     @pl.loop(0, D // T)
     def _(i):
         cc = cols(i, T)
-        part_s[:, cc] = mm_nt(gpu[oth, :], wup[cc, :]).astype(BF)
+        part_s[:, cc] = up_back(oth, cc).astype(BF)
 
     x_gn2 = xcopy(4, part_s, gn2_r)
     x_gn2.start()
@@ -1195,9 +1194,9 @@
     @pl.loop(0, D // T)
     def _(i):
         cc = cols(i, T)
-        own_f[:, cc] = mm_nt(gpu[own, :], wup[cc, :])
-        ffn_s[:, cc] = mm(up[oth, :], wdn[:, cc]).astype(BF)
-        ffn_o[:, cc] = mm(up[own, :], wdn[:, cc])
+        own_f[:, cc] = up_back(own, cc)
+        ffn_s[:, cc] = mm(up[oth, :], wdn[i // 2, :, cols(i % 2, T)]).astype(BF)
+        ffn_o[:, cc] = mm(up[own, :], wdn[i // 2, :, cols(i % 2, T)])
 
 
     pl.semaphore_signal(ready.at[0], inc=1, device_id=(wy, x), device_id_type=MESH)
@@ -1556,18 +1555,14 @@
     outs = (
         jax.ShapeDtypeStruct((H, D), BF),
         jax.ShapeDtypeStruct((H, D), F32),
-        jax.ShapeDtypeStruct((FL, D), BF),
-        jax.ShapeDtypeStruct((D, FL), BF),
-        jax.ShapeDtypeStruct((VL, D), BF),
+        jax.ShapeDtypeStruct((2, 7, D, P2), BF),
         jax.ShapeDtypeStruct((4, D, P2), BF),
-        jax.ShapeDtypeStruct((D, VL), BF),
-        jax.ShapeDtypeStruct((D, VL), BF),
         jax.ShapeDtypeStruct((D, Z), F32),
         jax.ShapeDtypeStruct((352, 128), F32),
     )
     dma = pltpu.SemaphoreType.DMA
     scratch = [
-        vm((D, Z), BF), vm((D, VL), BF), vm((D, VL), BF), vm((VL, D), BF), vm((D, D), BF), vm((D, D), BF), vm((D, FL), BF), vm((FL, D), BF),
+        vm((D, Z), BF), vm((D, VL), BF), vm((D, VL), BF), vm((VL, D), BF), vm((D, D), BF), vm((D, D), BF), vm((FL // P2, D, P2), BF), vm((2, FL, P2), BF),
         vm((R, D), BF), vm((R, D), BF), vm((R, D)), vm((R, D), BF), vm((R, D), BF), vm((R, D)), vm((R * 8, 128)), vm((R * 8, 128)),
         vm((R, Z)), vm((R, Z), BF), vm((R, Z), BF), vm((R, BLOCK)), vm((R, BLOCK), BF),
         vm((R, VL)), vm((R, VL)), vm((R, VL)), vm((R, VL), BF), vm((R, VL), BF), vm((H, D), BF), vm((H, D), BF), vm((H, D)), vm((H, D)), vm((H, D)), vm((H, D)), vm((R, D), BF),
@@ -1575,14 +1570,14 @@
         vm((H, D), BF), vm((H, D), BF), vm((H, D), BF),
         vm((R, D), BF), vm((R, D), BF), vm((R, D), BF), vm((R, FL // 2), BF), vm((R, D), BF), vm((R, FL // 2), BF), vm((R, VL), BF), vm((R, D), BF), vm((R, D), BF), vm((R, VL // 2), BF), vm((R, VL // 2), BF), vm((R, Z), BF),
         vm((128, 128)), vm((128, 128)), vm((128, 128)), vm((128, 128)), vm((128, 128)), vm((128, 128)), vm((24, D)), vm((R, 128)), vm((R, 128)), vm((R, 128)), vm((8, D)), vm((8, FL)),
-        vm((8, D, P2), BF), vm((11 * 256, P2), BF), vm((352, 128)), vm((3, 88, 128)), vm((344, 128)), vm((344, 128)), vm((NZ - 1, 344, 128)),
-        dma((10,)), dma((23,)), dma((23,)), dma((12,)), dma((12,)), dma((96,)), dma((SEMS,)), dma((SEMS,)), pltpu.SemaphoreType.REGULAR((3,)),
+        vm((8, D, P2), BF), vm((1, 11 * 256, P2), BF), vm((352, 128)), vm((3, 88, 128)), vm((344, 128)), vm((344, 128)), vm((NZ - 1, 344, 128)),
+        dma((14,)), dma((23,)), dma((23,)), dma((12,)), dma((12,)), dma((96,)), dma((SEMS,)), dma((SEMS,)), pltpu.SemaphoreType.REGULAR((3,)),
     ]
     return pl.pallas_call(
         main_kernel,
         out_shape=outs,
         in_specs=[anyspec] * 10 + [sspec, sspec] + [vspec] * 14,
-        out_specs=(vspec, vspec) + (anyspec,) * 6 + (vspec, vspec),
+        out_specs=(vspec, vspec) + (anyspec,) * 2 + (vspec, vspec),
         scratch_shapes=scratch,
         compiler_params=pltpu.CompilerParams(collective_id=0, has_side_effects=True, vmem_limit_bytes=63 * 1024 * 1024),
         cost_estimate=pl.CostEstimate(flops=15_000_000_000, bytes_accessed=40_000_000, transcendentals=0),
@@ -1593,27 +1588,37 @@
     )
 
 
-def finish_kernel(down, up, mix, reset, value, hu, bo, gt, shared, small, rate, damp, ein, eout, bmap,
+def finish_kernel(every, hu, bo, gt, shared, small, rate, damp, ein, eout, bmap,
                   f_down, f_up, f_mix, f_reset, f_value, f_hid, f_upd, f_bo, f_gt, f_shared,
                   g_rate, g_damp, g_in, g_out, v0, v1, v2, v3, v4, v5, g_bup, g_gain, g_bias, g_rel,
-                  b_down, b_up, b_mix, b_reset, b_value, b_hu, b_bo, b_gt, b_shared, stage, isem, osem, psem):
+                  b_every, b_hu, b_bo, b_gt, b_shared, stage, isem, osem, psem):
     rows_in = [pltpu.make_async_copy(a, b, psem.at[k]) for k, (a, b) in enumerate(((bo, b_bo), (gt, b_gt), (shared, b_shared)))]
     passed = [pltpu.make_async_copy(a, b, psem.at[3 + k]) for k, (a, b) in enumerate(((b_bo, f_bo), (b_gt, f_gt), (b_shared, f_shared)))]
     CR, CC = stage.shape[1], stage.shape[2]
+    half = CC // 2
     chunks = []
-    for src, buf, dst in ((down, b_down, f_down), (up, b_up, f_up), (mix, b_mix, f_mix), (reset, b_reset, f_reset), (value, b_value, f_value)):
-        for r in range(src.shape[0] // CR):
-            for q in range(src.shape[1] // CC):
-                at = (slice(r * CR, (r + 1) * CR), slice(q * CC, (q + 1) * CC))
-                chunks.append(([(src.at[at], buf.at[at], slice(0, CC))], dst.at[at]))
-    half = CC // 2
+
+    def gather(sources, dst):
+        chunks.append(([(a, b, slice(j * half, (j + 1) * half)) for j, (a, b) in enumerate(sources)], dst))
+
+    def piece(core, i, r):
+        at = (core, i, slice(r * CR, (r + 1) * CR))
+        return every.at[at], b_every.at[at]
+
+    def quarter(q, n):
+        at = (q, slice(n * CR, (n + 1) * CR))
+        return hu.at[at], b_hu.at[at]
+
+    for core in range(2):
+        for r in range(4):
+            gather([piece(core, 0, r), piece(core, 1, r)], f_down.at[core * 4 * CR + r * CR : core * 4 * CR + (r + 1) * CR])
+            gather([piece(core, 2, r), piece(core, 3, r)], f_up.at[r * CR : (r + 1) * CR, core * CC : (core + 1) * CC])
+    for i, dst in ((4, f_mix), (5, f_reset), (6, f_value)):
+        for r in range(4):
+            gather([piece(0, i, r), piece(1, i, r)], dst.at[r * CR : (r + 1) * CR])
     for n, dst in ((0, f_hid), (2, f_upd)):
         for q in range(4):
-            parts = []
-            for j in range(2):
-                at = (q, slice((n + j) * CR, (n + j + 1) * CR))
-                parts.append((hu.at[at], b_hu.at[at], slice(j * half, (j + 1) * half)))
-            chunks.append((parts, dst.at[q * CR : (q + 1) * CR]))
+            gather([quarter(q, n), quarter(q, n + 1)], dst.at[q * CR : (q + 1) * CR])
     ins, count = [], 0
     for parts, _ in chunks:
         ins.append([])
@@ -1673,11 +1678,11 @@
         copy.wait()
 
 
-def run_finish(grads, hu, whole, small, rate, damp, ein, eout, bucket_map, nbuck):
+def run_finish(every, hu, whole, shapes, small, rate, damp, ein, eout, bucket_map, nbuck):
     bmap = bucket_map.reshape(1, -1)
     D = rate.shape[1]
     square = jax.ShapeDtypeStruct((D, D), F32)
-    outs = [jax.ShapeDtypeStruct(a.shape, F32) for a in grads] + [square, square]
+    outs = [jax.ShapeDtypeStruct(a.shape, F32) for a in shapes] + [square, square]
     outs += [jax.ShapeDtypeStruct(a.shape, a.dtype) for a in whole]
     kept = len(outs)
     outs += [jax.ShapeDtypeStruct(rate.shape, F32) for _ in range(4)]
@@ -1691,21 +1696,23 @@
     res = pl.pallas_call(
         finish_kernel,
         out_shape=tuple(outs),
-        in_specs=[anyspec] * (len(grads) + 4) + [vspec] * 6,
+        in_specs=[anyspec] * 5 + [vspec] * 6,
         out_specs=tuple([anyspec] * kept + [vspec] * (len(outs) - kept)),
-        scratch_shapes=[vm(a.shape, BF) for a in grads] + [vm(hu.shape, BF)] + [vm(a.shape, a.dtype) for a in whole] + [vm((ring, D // 4, D)), dma((44,)), dma((ring,)), dma((6,))],
+        scratch_shapes=[vm(every.shape, BF), vm(hu.shape, BF)] + [vm(a.shape, a.dtype) for a in whole] + [vm((ring, D // 4, D)), dma((72,)), dma((ring,)), dma((6,))],
         compiler_params=pltpu.CompilerParams(vmem_limit_bytes=60 * 1024 * 1024),
-    )(*grads, hu, *whole, small, rate, damp, ein, eout, bmap)
+    )(every, hu, *whole, small, rate, damp, ein, eout, bmap)
     return res
 
 
 def shards_fast(*args):
-    bo, gt, down, up, mix, hu, reset, value, shared, small = run_main(*args)
+    bo, gt, every, hu, shared, small = run_main(*args)
+    w_value, w_reset, w_mix = args[15:18]
+    w_up, w_down = args[23], args[25]
     (tokens, cotangent, seq_lengths, bucket_map, norm1_gain, norm1_bias, ema_rate, ema_damp, ema_in, ema_out,
      ema_skip, w_shared, qk_gain, qk_bias, rel_bias) = args[:15]
     (down, up, mix, reset, value, hidden, update, bo, gt, shared, g_rate, g_damp, g_in, g_out, skip, n1g, n1b, bupd, n2g, n2b,
      g_bup, g_gain, g_bias, g_rel) = run_finish(
-        (down, up, mix, reset, value), hu, (bo, gt, shared), small, ema_rate, ema_damp, ema_in, ema_out, bucket_map,
+        every, hu, (bo, gt, shared), (w_down, w_up, w_mix, w_reset, w_value), small, ema_rate, ema_damp, ema_in, ema_out, bucket_map,
         rel_bias.shape[0])
     skip, n1g, n1b, bupd, n2g, n2b = [v.reshape(-1) for v in (skip, n1g, n1b, bupd, n2g, n2b)]
     return (bo, gt, n1g, n1b, g_rate, g_damp, g_in, g_out, skip, shared, g_gain, g_bias, g_rel.reshape(-1),

time: 222 us -> 223 us (level)
  no operation moved by 1% of the time
where the time goes in v2:
time: 223 us
  Pallas kernels  222 us (100%)
    pallas_call x1, Pallas kernels, run_main(): pl.pallas_call(main_kernel, out_shape=outs, in_specs=[anyspec] * 10 + [ss...  201 us
    pallas_call x1, Pallas kernels, run_finish(): pl.pallas_call(finish_kernel, out_shape=tuple(outs), in_specs=[anyspec] *...  21.4 us

profile of v2, /device:TPU:1, one launch (start us, length us, event | category | flops | bytes accessed | tf_op | source)
XLA Modules:
  0.0 222.8 jit_solution(12630834029544806581)
XLA Ops:
  0.7 200.5 %shard_map.433 = (bf16[128,1024]{1,0:T(8,128)(2,1)}, f32[128,1024]{1,0:T(8,128)}, bf16[2,7,1024,512]{3,2,1,0:T(8,128)(2,1)}, bf16[4,1024,512]{2,1,0:T(8,128)(2,1...) custom-call(bf16[128,1024]{1,0:T(8,128)(2,1)} %tok_h.1, bf16[128,1024]{1,0:T(8,128)(2,1)} %cot_h.1, bf16[1024,128]{1,0:T(8,128)(2,1)} %wsh_h.1, ...), custom_call_target="tpu_custom_call" | custom-call | flops 15000000512 | bytes 40000000 | tf_op jit(solution)/shard_map/pallas_call | solution.py:1576
  201.2 21.4 %shard_map.434 = (f32[2048,1024]{1,0:T(8,128)}, f32[1024,2048]{1,0:T(8,128)}, f32[1024,1024]{1,0:T(8,128)}, f32[1024,1024]{1,0:T(8,128)}, f32[1024,1024]{1,0:T(8...) custom-call(bf16[2,7,1024,512]{3,2,1,0:T(8,128)(2,1)} %get-tuple-ele, ...), custom_call_target="tpu_custom_call" | custom-call | tf_op jit(solution)/shard_map/pallas_call | solution.py:1696

commit v3 on v2

--- a/solution.py
+++ b/solution.py
@@ -748,9 +748,7 @@
         copy.wait_send()
     x_cot.start()
     c_normed = ccopy(0, nlow, p_normed)
-    c_normed.start()
     c_mixed = ccopy(1, mlow, p_mixed)
-    c_mixed.start()
 
     wcopies[2].wait()
     psh = mm(mlow[...], wsh[...])
@@ -816,7 +814,6 @@
         x_mix[h].start()
 
     c_gated = ccopy(2, gated, p_gated)
-    c_gated.start()
     wcopies[6].wait()
     wcopies[7].wait()
 
@@ -891,15 +888,15 @@
     for copy in x_n2:
         copy.wait()
     c_n2 = ccopy(4, n2, p_n2)
-    c_n2.start()
     halfF = FL // 2
     theirs_f = pl.ds(pl.multiple_of((1 - c) * halfF, halfF), halfF)
     pl.loop(0, FT // 2, unroll=2)(lambda i: up_tile((1 - c) * (FT // 2) + i, oth, False))
     c_up = ccopy(5, up.at[:, theirs_f], p_up)
     c_gpu = ccopy(6, gpu.at[:, theirs_f], p_gpu)
     c_up.start()
+    pl.loop(0, FT // 2, unroll=2)(lambda i: up_tile(c * (FT // 2) + i, oth, False))
     c_gpu.start()
-    pl.loop(0, FT // 2, unroll=2)(lambda i: up_tile(c * (FT // 2) + i, oth, False))
+    c_n2.start()
     P2 = g_v.shape[2]
     plan = make_plan()[0]
     numbers = {}
@@ -1233,6 +1230,9 @@
             nn = slice(j * P2, (j + 1) * P2)
             g_v[2 + j, mt, :] = (mm_tn(la, gpu[:, nf]) + mm_tn(lb, p_gpu[:, nn])).astype(BF)
 
+    c_gated.start()
+    c_mixed.start()
+    c_normed.start()
     slot(4)
     x_gn2.wait()
 

time: 223 us -> 223 us (level)
  no operation moved by 1% of the time
where the time goes in v3:
time: 223 us
  Pallas kernels  222 us (100%)
    pallas_call x1, Pallas kernels, run_main(): pl.pallas_call(main_kernel, out_shape=outs, in_specs=[anyspec] * 10 + [ss...  201 us
    pallas_call x1, Pallas kernels, run_finish(): pl.pallas_call(finish_kernel, out_shape=tuple(outs), in_specs=[anyspec] *...  21.4 us

profile of v3, /device:TPU:1, one launch (start us, length us, event | category | flops | bytes accessed | tf_op | source)
XLA Modules:
  0.0 222.7 jit_solution(1820847784062953855)
XLA Ops:
  0.7 200.5 %shard_map.433 = (bf16[128,1024]{1,0:T(8,128)(2,1)}, f32[128,1024]{1,0:T(8,128)}, bf16[2,7,1024,512]{3,2,1,0:T(8,128)(2,1)}, bf16[4,1024,512]{2,1,0:T(8,128)(2,1...) custom-call(bf16[128,1024]{1,0:T(8,128)(2,1)} %tok_h.1, bf16[128,1024]{1,0:T(8,128)(2,1)} %cot_h.1, bf16[1024,128]{1,0:T(8,128)(2,1)} %wsh_h.1, ...), custom_call_target="tpu_custom_call" | custom-call | flops 15000000512 | bytes 40000000 | tf_op jit(solution)/shard_map/pallas_call | solution.py:1576
  201.2 21.4 %shard_map.434 = (f32[2048,1024]{1,0:T(8,128)}, f32[1024,2048]{1,0:T(8,128)}, f32[1024,1024]{1,0:T(8,128)}, f32[1024,1024]{1,0:T(8,128)}, f32[1024,1024]{1,0:T(8...) custom-call(bf16[2,7,1024,512]{3,2,1,0:T(8,128)(2,1)} %get-tuple-ele, ...), custom_call_target="tpu_custom_call" | custom-call | tf_op jit(solution)/shard_map/pallas_call | solution.py:1696

commit v4 on v3

--- a/solution.py
+++ b/solution.py
@@ -407,7 +407,7 @@
     (4, 1, 0, 1024, MIXED), (5, 0, 0, 512, MIXED), (5, 0, 512, 512, MIXED), (6, 1, 0, 256, EVEN), (6, 2, 256, 768, ENDS),
     (7, 1, 0, 512, ENDS), (7, 1, 512, 512, ENDS),
 )
-PHASES = (1.8, 1.2, 2.4, 1.8, 4.2, 1.4, 6.6, 1.8, 1.8, 1.8, 1.2, 1.2, 1.0, 1.8, 1.0, 2.4, 1.0, 1.2, 2.4, 1.6, 1.6, 1.6, 1.6, 4.8, 1.2)
+PHASES = (2.2, 1.5, 3.0, 2.2, 5.2, 1.8, 8.2, 2.2, 2.2, 2.2, 1.5, 1.5, 1.2, 2.2, 1.2, 3.0, 1.2, 1.5, 3.0, 2.0, 2.0, 2.0, 2.0, 6.0, 1.5)
 RELEASE = {0: 0, 1: 0, 2: 3, 3: 3, 4: 12, 5: 14, 6: 16, 7: 17}
 EARLY = tuple(u for u, t in enumerate(UNITS) if t[0] < 2)
 UNIT, LAG = 3.0, 2.0

time: 223 us -> 222 us (level)
  no operation moved by 1% of the time
where the time goes in v4:
time: 222 us
  Pallas kernels  221 us (100%)
    pallas_call x1, Pallas kernels, run_main(): pl.pallas_call(main_kernel, out_shape=outs, in_specs=[anyspec] * 10 + [ss...  200 us
    pallas_call x1, Pallas kernels, run_finish(): pl.pallas_call(finish_kernel, out_shape=tuple(outs), in_specs=[anyspec] *...  21.4 us

profile of v4, /device:TPU:1, one launch (start us, length us, event | category | flops | bytes accessed | tf_op | source)
XLA Modules:
  0.0 221.9 jit_solution(15646418328904383679)
XLA Ops:
  0.7 199.7 %shard_map.433 = (bf16[128,1024]{1,0:T(8,128)(2,1)}, f32[128,1024]{1,0:T(8,128)}, bf16[2,7,1024,512]{3,2,1,0:T(8,128)(2,1)}, bf16[4,1024,512]{2,1,0:T(8,128)(2,1...) custom-call(bf16[128,1024]{1,0:T(8,128)(2,1)} %tok_h.1, bf16[128,1024]{1,0:T(8,128)(2,1)} %cot_h.1, bf16[1024,128]{1,0:T(8,128)(2,1)} %wsh_h.1, ...), custom_call_target="tpu_custom_call" | custom-call | flops 15000000512 | bytes 40000000 | tf_op jit(solution)/shard_map/pallas_call | solution.py:1576
  200.4 21.4 %shard_map.434 = (f32[2048,1024]{1,0:T(8,128)}, f32[1024,2048]{1,0:T(8,128)}, f32[1024,1024]{1,0:T(8,128)}, f32[1024,1024]{1,0:T(8,128)}, f32[1024,1024]{1,0:T(8...) custom-call(bf16[2,7,1024,512]{3,2,1,0:T(8,128)(2,1)} %get-tuple-ele, ...), custom_call_target="tpu_custom_call" | custom-call | tf_op jit(solution)/shard_map/pallas_call | solution.py:1696
